TPU v7x, 32 devices: a whole 2x2x4 slice. The times are simulated.
32 devices in a mesh: dp: 8 (over z, y), tensor: 4 (over x, core).
Axes of the slice: x: 2, y: 2, z: 4, core: 2. Of those that a mesh axis runs over, the one named last changes fastest.
Arguments:
- layer_in: float32 [4096, 1024], P('dp', 'tensor'), may hold values from -18 to 18
- cotangent: float32 [4096, 1024], P('dp', 'tensor'), may hold values from -6 to 6
- segment_ids: int32 [8, 512], P('dp'), may hold values from 0 to 2, never falling along the last dimension, each value on 1 to 256 neighbouring positions
- owner_map: int32 [2, 192], replicated, may hold values from 0 to 191, as said below
- masters: float32 [2, 768, 128, 128], P(None, ('dp', 'tensor')), may hold values from -0.375 to 0.375
- left_stats: float32 [2, 768, 128, 128], P(None, ('dp', 'tensor')), may hold values from -524288 to 524288, as said below
- right_stats: float32 [2, 768, 128, 128], P(None, ('dp', 'tensor')), may hold values from -524288 to 524288, as said below
- left_roots: float32 [2, 768, 128, 128], P(None, ('dp', 'tensor')), may hold values from -0.13834965 to 0.13834965, as said below
- right_roots: float32 [2, 768, 128, 128], P(None, ('dp', 'tensor')), may hold values from -0.13834965 to 0.13834965, as said below
- vectors: float32 [2, 8, 1024], P(None, None, 'tensor'), may hold values from -1.5 to 2.5, as said below
- up_bias: float32 [2, 4096], P(None, 'tensor'), may hold values from -1.5 to 1.5
Outputs:
- layer_out: float32 [4096, 1024], P('dp', 'tensor')
- input_grad: float32 [4096, 1024], P('dp', 'tensor')
- weight_grads: float32 [2, 768, 128, 128], P(None, ('dp', 'tensor'))
- new_left: float32 [2, 768, 128, 128], P(None, ('dp', 'tensor'))
- new_right: float32 [2, 768, 128, 128], P(None, ('dp', 'tensor'))
- new_weights: float32 [2, 768, 128, 128], P(None, ('dp', 'tensor'))
- vector_grads: float32 [2, 8, 1024], P(None, None, 'tensor')
- vectors_new: float32 [2, 8, 1024], P(None, None, 'tensor')
- up_bias_grads: float32 [2, 4096], P(None, 'tensor')
- up_bias_new: float32 [2, 4096], P(None, 'tensor')
Inputs may be any that keep to these rules, and one draw needn't show every extreme that they name: `segment_ids`: ids do not fall along a row; each id names one run of at most 256 positions of its row. For each layer a permutation of 0 to 191; block b of an index of tensor is held by index owner_map // 24 of dp in slot owner_map % 24. `left_stats`: Symmetric. `right_stats`: Symmetric. `left_roots`: Symmetric. `right_roots`: Symmetric. `vectors`: gains are positive.
All inputs are finite; a program needn't handle non-finite values.
Results may differ from a plain program's by a relative error of at most 0.033.
The roundings to bfloat16 on the way count: a program that leaves them out, or rounds other values in their place, can miss the bound.
Values may be sent and summed in bfloat16 or wider, within the bound.
No kernel may reach another device: no remote copies, remote signals or barrier semaphores. Data moves between devices by JAX's collectives and lax.ppermute only.
A program may use at most 192 MiB of HBM per device.

v0:
```python
import math

import jax
import jax.numpy as jnp
from jax import lax
from jax.sharding import PartitionSpec as P

HD = 64


eps_norm = 1e-12
stat_decay = 0.5
update_rate = 0.5


def unblock(blocks, rows_total, cols_total):
    block_size = blocks.shape[-1]
    tiled = blocks.reshape(
        rows_total // block_size, cols_total // block_size, block_size, block_size
    )
    return tiled.transpose(0, 2, 1, 3).reshape(rows_total, cols_total)


def to_blocks(matrix, block_size):
    rows_total, cols_total = matrix.shape
    tiled = matrix.reshape(
        rows_total // block_size, block_size, cols_total // block_size, block_size
    )
    return tiled.transpose(0, 2, 1, 3).reshape(-1, block_size, block_size)


def widen(values):
    return lax.all_gather(values.astype(jnp.bfloat16), "tensor", axis=1, tiled=True)


def branch_total(partial_value):
    return lax.psum_scatter(partial_value, "tensor", scatter_dimension=1, tiled=True)


def widen_grad(values):
    return lax.all_gather(values.astype(jnp.bfloat16), "tensor", axis=1, tiled=True)


def grad_total(partial_value):
    return lax.psum_scatter(
        partial_value.astype(jnp.bfloat16), "tensor", scatter_dimension=1, tiled=True
    ).astype(jnp.float32)


def norm_forward(hidden, model_width):
    center = lax.psum(jnp.sum(hidden, axis=1), "tensor") / model_width
    centred = hidden - center[:, None]
    spread = lax.psum(jnp.sum(centred * centred, axis=1), "tensor") / model_width
    inv_scale = lax.rsqrt(spread + eps_norm)
    return ((hidden - center[:, None]) * inv_scale[:, None], inv_scale)


def norm_back(grad_out, normed, inv_scale, gain_row, model_width):
    scaled_grad = grad_out * gain_row
    sum_grad, sum_cross = lax.psum(
        (jnp.sum(scaled_grad, axis=1), jnp.sum(scaled_grad * normed, axis=1)), "tensor"
    )
    grad_in = inv_scale[:, None] * (
        scaled_grad - (sum_grad[:, None] + normed * sum_cross[:, None]) / model_width
    )
    return (grad_in, jnp.sum(grad_out * normed, axis=0), jnp.sum(grad_out, axis=0))


def masked_scores(query, key_rows, allowed):
    score_scale = query.shape[-1] ** (-0.5)
    scores = (
        jnp.einsum("shd,khd->hsk", query, key_rows, preferred_element_type=jnp.float32)
        * score_scale
    )
    return (jnp.where(allowed[None], scores, -1e30), score_scale)


def attend_row(packed):
    query, key_rows, values, allowed = packed
    scores, score_scale = masked_scores(query, key_rows, allowed)
    row_max = jnp.max(scores, axis=-1, keepdims=True)
    exponent = jnp.exp(scores - row_max)
    row_total = jnp.sum(exponent, axis=-1, keepdims=True)
    attention = (exponent / row_total).astype(jnp.bfloat16)
    mixture = jnp.einsum("hsk,khd->shd", attention, values, preferred_element_type=jnp.float32)
    return (mixture.astype(jnp.bfloat16), row_max[..., 0] + jnp.log(row_total[..., 0]))


def attend_back(packed):
    query, key_rows, values, allowed, log_total, grad_mix = packed
    scores, score_scale = masked_scores(query, key_rows, allowed)
    attention = jnp.exp(scores - log_total[..., None])
    grad_values = jnp.einsum(
        "hsk,shd->khd", attention.astype(jnp.bfloat16), grad_mix, preferred_element_type=jnp.float32
    )
    grad_attention = jnp.einsum(
        "shd,khd->hsk", grad_mix, values, preferred_element_type=jnp.float32
    )
    row_inner = jnp.sum(attention * grad_attention, axis=-1, keepdims=True)
    grad_scores = (attention * (grad_attention - row_inner)).astype(jnp.bfloat16)
    grad_query = (
        jnp.einsum("hsk,khd->shd", grad_scores, key_rows, preferred_element_type=jnp.float32)
        * score_scale
    )
    grad_keys = (
        jnp.einsum("hsk,shd->khd", grad_scores, query, preferred_element_type=jnp.float32)
        * score_scale
    )
    return (
        grad_query.astype(jnp.bfloat16),
        grad_keys.astype(jnp.bfloat16),
        grad_values.astype(jnp.bfloat16),
    )


def forward_layer(hidden_in, weight_set, vector_rows, up_row, allowed):
    qkv_weight, out_weight, up_weight, down_weight = weight_set
    tokens_here, width_part = hidden_in.shape
    model_width = qkv_weight.shape[0]
    head_shape = (allowed.shape[0], allowed.shape[1], width_part // HD, HD)
    wide_in = widen(hidden_in)
    projected = jnp.dot(wide_in, qkv_weight, preferred_element_type=jnp.float32)
    query = (projected[:, :width_part] + vector_rows[0]).astype(jnp.bfloat16)
    key_rows = projected[:, width_part : 2 * width_part].astype(jnp.bfloat16)
    values = (projected[:, 2 * width_part :] + vector_rows[1]).astype(jnp.bfloat16)
    mixture, log_total = lax.map(
        attend_row,
        (
            query.reshape(head_shape),
            key_rows.reshape(head_shape),
            values.reshape(head_shape),
            allowed,
        ),
    )
    mixture = mixture.reshape(tokens_here, width_part)
    first_sum = (
        hidden_in
        + branch_total(jnp.dot(mixture, out_weight, preferred_element_type=jnp.float32))
        + vector_rows[2]
    )
    normed_first, scale_first = norm_forward(first_sum, model_width)
    middle = normed_first * vector_rows[3] + vector_rows[4]
    wide_mid = widen(middle)
    pre_act = jnp.dot(wide_mid, up_weight, preferred_element_type=jnp.float32) + up_row
    activated = jax.nn.gelu(pre_act, approximate=False).astype(jnp.bfloat16)
    second_sum = (
        middle
        + branch_total(jnp.dot(activated, down_weight, preferred_element_type=jnp.float32))
        + vector_rows[5]
    )
    normed_second, scale_second = norm_forward(second_sum, model_width)
    result = normed_second * vector_rows[6] + vector_rows[7]
    kept_values = (
        wide_in,
        query,
        key_rows,
        values,
        log_total,
        mixture,
        normed_first,
        scale_first,
        wide_mid,
        pre_act,
        activated,
        normed_second,
        scale_second,
    )
    return (result, kept_values)


def backward_layer(grad_result, kept_values, weight_set, vector_rows, allowed):
    (
        wide_in,
        query,
        key_rows,
        values,
        log_total,
        mixture,
        normed_first,
        scale_first,
        wide_mid,
        pre_act,
        activated,
        normed_second,
        scale_second,
    ) = kept_values
    qkv_weight, out_weight, up_weight, down_weight = weight_set
    model_width = qkv_weight.shape[0]
    tokens_here, width_part = mixture.shape
    head_shape = (allowed.shape[0], allowed.shape[1], width_part // HD, HD)
    grad_second, gain_two, shift_two = norm_back(
        grad_result, normed_second, scale_second, vector_rows[6], model_width
    )
    wide_grad = widen_grad(grad_second)
    down_grad = jnp.einsum("tf,td->fd", activated, wide_grad, preferred_element_type=jnp.float32)
    grad_activ = jnp.einsum("td,fd->tf", wide_grad, down_weight, preferred_element_type=jnp.float32)
    _, gelu_pull = jax.vjp(lambda inner_value: jax.nn.gelu(inner_value, approximate=False), pre_act)
    grad_pre = gelu_pull(grad_activ)[0].astype(jnp.bfloat16)
    up_grad = jnp.einsum("td,tf->df", wide_mid, grad_pre, preferred_element_type=jnp.float32)
    grad_middle = grad_second + grad_total(
        jnp.einsum("tf,df->td", grad_pre, up_weight, preferred_element_type=jnp.float32)
    )
    grad_first, gain_one, shift_one = norm_back(
        grad_middle, normed_first, scale_first, vector_rows[3], model_width
    )
    wide_first = widen_grad(grad_first)
    out_grad = jnp.einsum("tc,td->cd", mixture, wide_first, preferred_element_type=jnp.float32)
    grad_mix = jnp.einsum(
        "td,cd->tc", wide_first, out_weight, preferred_element_type=jnp.float32
    ).astype(jnp.bfloat16)
    grad_query, grad_keys, grad_values = lax.map(
        attend_back,
        (
            query.reshape(head_shape),
            key_rows.reshape(head_shape),
            values.reshape(head_shape),
            allowed,
            log_total,
            grad_mix.reshape(head_shape),
        ),
    )
    grad_qkv = jnp.concatenate(
        [
            grad_query.reshape(tokens_here, width_part),
            grad_keys.reshape(tokens_here, width_part),
            grad_values.reshape(tokens_here, width_part),
        ],
        axis=1,
    )
    qkv_grad = jnp.einsum("td,tc->dc", wide_in, grad_qkv, preferred_element_type=jnp.float32)
    grad_in = grad_first + grad_total(
        jnp.einsum("tc,dc->td", grad_qkv, qkv_weight, preferred_element_type=jnp.float32)
    )
    query_bias = jnp.sum(grad_qkv[:, :width_part].astype(jnp.float32), axis=0)
    value_bias = jnp.sum(grad_qkv[:, 2 * width_part :].astype(jnp.float32), axis=0)
    vector_grad = jnp.stack(
        [
            query_bias,
            value_bias,
            jnp.sum(grad_first, axis=0),
            gain_one,
            shift_one,
            jnp.sum(grad_second, axis=0),
            gain_two,
            shift_two,
        ]
    )
    up_bias_grad = jnp.sum(grad_pre.astype(jnp.float32), axis=0)
    return (grad_in, (qkv_grad, out_grad, up_grad, down_grad), vector_grad, up_bias_grad)


def body(
    layer_in,
    cotangent,
    segment_ids,
    owner_map,
    masters,
    left_stats,
    right_stats,
    left_roots,
    right_roots,
    vectors,
    up_bias,
):
    layer_count = masters.shape[0]
    block_size = masters.shape[-1]
    tokens_here, width_part = layer_in.shape
    model_width = width_part * lax.axis_size("tensor")
    ff_part = up_bias.shape[1]
    copies = lax.all_gather(masters.astype(jnp.bfloat16), "dp", axis=1, tiled=True)
    tile_rows = model_width // block_size
    n_qkv = tile_rows * (3 * width_part // block_size)
    n_out = width_part // block_size * tile_rows
    n_up = tile_rows * (ff_part // block_size)
    weight_sets = []
    for layer_idx in range(layer_count):
        blocks = jnp.take(copies[layer_idx], owner_map[layer_idx], axis=0)
        weight_sets.append(
            (
                unblock(blocks[:n_qkv], model_width, 3 * width_part),
                unblock(blocks[n_qkv : n_qkv + n_out], width_part, model_width),
                unblock(blocks[n_qkv + n_out : n_qkv + n_out + n_up], model_width, ff_part),
                unblock(blocks[n_qkv + n_out + n_up :], ff_part, model_width),
            )
        )
    allowed = segment_ids[:, :, None] == segment_ids[:, None, :]
    hidden_now = layer_in
    kept_all = []
    for layer_idx in range(layer_count):
        hidden_now, kept_values = forward_layer(
            hidden_now, weight_sets[layer_idx], vectors[layer_idx], up_bias[layer_idx], allowed
        )
        kept_all.append(kept_values)
    inverse = jnp.argsort(owner_map, axis=1)
    grad_now = cotangent
    placed_all = [None] * layer_count
    vector_all = [None] * layer_count
    up_all = [None] * layer_count
    for layer_idx in reversed(range(layer_count)):
        grad_now, matrix_grads, vector_grad, up_grad = backward_layer(
            grad_now, kept_all[layer_idx], weight_sets[layer_idx], vectors[layer_idx], allowed
        )
        block_grads = jnp.concatenate(
            [
                to_blocks(matrix_grads[0], block_size),
                to_blocks(matrix_grads[1], block_size),
                to_blocks(matrix_grads[2], block_size),
                to_blocks(matrix_grads[3], block_size),
            ],
            axis=0,
        )
        placed = jnp.take(block_grads, inverse[layer_idx], axis=0)
        placed_all[layer_idx] = placed
        vector_all[layer_idx] = vector_grad
        up_all[layer_idx] = up_grad
    reduced = lax.psum_scatter(jnp.stack(placed_all), "dp", scatter_dimension=1, tiled=True)
    vector_grads, up_bias_grads = lax.psum((jnp.stack(vector_all), jnp.stack(up_all)), "dp")
    precise = lax.Precision.HIGHEST
    left_new = stat_decay * left_stats + (1.0 - stat_decay) * jnp.einsum(
        "lkij,lkmj->lkim", reduced, reduced, precision=precise
    )
    right_new = stat_decay * right_stats + (1.0 - stat_decay) * jnp.einsum(
        "lkji,lkjm->lkim", reduced, reduced, precision=precise
    )
    right_side = jnp.einsum("lkij,lkjm->lkim", reduced, right_roots, precision=precise)
    precond = jnp.einsum("lkij,lkjm->lkim", left_roots, right_side, precision=precise)
    new_weights = masters - update_rate * precond
    vector_rate = 0.5 / math.sqrt(tokens_here * lax.axis_size("dp"))
    return (
        hidden_now,
        grad_now,
        reduced,
        left_new,
        right_new,
        new_weights,
        vector_grads,
        vectors - vector_rate * vector_grads,
        up_bias_grads,
        up_bias - vector_rate * up_bias_grads,
    )


def solution(mesh):
    return jax.shard_map(
        body,
        mesh=mesh,
        in_specs=(
            P("dp", "tensor"),
            P("dp", "tensor"),
            P("dp", None),
            P(),
            P(None, ("dp", "tensor"), None, None),
            P(None, ("dp", "tensor"), None, None),
            P(None, ("dp", "tensor"), None, None),
            P(None, ("dp", "tensor"), None, None),
            P(None, ("dp", "tensor"), None, None),
            P(None, None, "tensor"),
            P(None, "tensor"),
        ),
        out_specs=(
            P("dp", "tensor"),
            P("dp", "tensor"),
            P(None, ("dp", "tensor"), None, None),
            P(None, ("dp", "tensor"), None, None),
            P(None, ("dp", "tensor"), None, None),
            P(None, ("dp", "tensor"), None, None),
            P(None, None, "tensor"),
            P(None, None, "tensor"),
            P(None, "tensor"),
            P(None, "tensor"),
        ),
        check_vma=False,
    )
```

profile of v0, /device:TPU:0, one launch (start us, length us, event | category | flops | bytes accessed | tf_op | source)
XLA Modules:
  0.0 1338.0 jit_solution(9746463901671874512)
XLA Ops:
  13.0 177.1 %all-gather.10.cloned.1.call-done = bf16[2,192,128,128]{3,2,1,0:T(8,128)(2,1)} async-done(((bf16[2,24,128,128]{3,2,1,0:T(8,128)(2,1)}), bf16[2,192,128,128]{3,2,1,0:T(8,128)(2,1)}) %all-gather.10.cloned.1.call-update) | async-done | bytes 12582928 | tf_op jit(solution)/shard_map/all_gather | solution.py:270
  190.0 10.6 slice_bitcast_fusion
  200.7 10.8 gather_fusion
  231.4 29.7 %reduce-scatter.13.cloned.1.call-done = f32[512,256]{1,0:T(8,128)} async-done(((f32[512,1024]{1,0:T(8,128)}), f32[512,256]{1,0:T(8,128)}) %reduce-scatter.13.cloned.1.call-update) | async-done | bytes 524304 | tf_op jit(solution)/shard_map/reduce_scatter | solution.py:37
  286.2 9.9 all-gather.14.cloned.1.call-done
  296.1 9.0 multiply_convert_fusion.3
  308.7 31.5 %reduce-scatter.15.cloned.1.call-done = f32[512,256]{1,0:T(8,128)} async-done(((f32[512,1024]{1,0:T(8,128)}), f32[512,256]{1,0:T(8,128)}) %reduce-scatter.15.cloned.1.call-update) | async-done | bytes 524304 | tf_op jit(solution)/shard_map/reduce_scatter | solution.py:37
  357.4 10.8 gather_fusion.1
  396.0 32.9 %reduce-scatter.17.cloned.1.call-done = f32[512,256]{1,0:T(8,128)} async-done(((f32[512,1024]{1,0:T(8,128)}), f32[512,256]{1,0:T(8,128)}) %reduce-scatter.17.cloned.1.call-update) | async-done | bytes 524304 | tf_op jit(solution)/shard_map/reduce_scatter | solution.py:37
  454.5 9.6 all-gather.18.cloned.1.call-done
  464.1 9.0 multiply_convert_fusion.2
  476.8 31.5 %reduce-scatter.19.cloned.1.call-done = f32[512,256]{1,0:T(8,128)} async-done(((f32[512,1024]{1,0:T(8,128)}), f32[512,256]{1,0:T(8,128)}) %reduce-scatter.19.cloned.1.call-update) | async-done | bytes 524304 | tf_op jit(solution)/shard_map/reduce_scatter | solution.py:37
  525.3 6.8 all-reduce.4
  534.8 17.3 %all-gather.20.cloned.1.call-done = bf16[512,1024]{1,0:T(8,128)(2,1)} async-done(((bf16[512,256]{1,0:T(8,128)(2,1)}), bf16[512,1024]{1,0:T(8,128)(2,1)}) %all-gather.20.cloned.1.call-update) | async-done | bytes 1048592 | tf_op jit(solution)/shard_map/all_gather | solution.py:41
  561.5 24.8 %reduce-scatter.21.cloned.1.call-done = bf16[512,256]{1,0:T(8,128)(2,1)} async-done(((bf16[512,1024]{1,0:T(8,128)(2,1)}), bf16[512,256]{1,0:T(8,128)(2,1)}) %reduce-scatter.21.cloned.1.call-update) | async-done | bytes 262160 | tf_op jit(solution)/shard_map/reduce_scatter | solution.py:45
  596.9 18.0 %all-gather.22.cloned.1.call-done = bf16[512,1024]{1,0:T(8,128)(2,1)} async-done(((bf16[512,256]{1,0:T(8,128)(2,1)}), bf16[512,1024]{1,0:T(8,128)(2,1)}) %all-gather.22.cloned.1.call-update) | async-done | bytes 1048592 | tf_op jit(solution)/shard_map/all_gather | solution.py:41
  627.5 25.0 %reduce-scatter.23.cloned.1.call-done = bf16[512,256]{1,0:T(8,128)(2,1)} async-done(((bf16[512,1024]{1,0:T(8,128)(2,1)}), bf16[512,256]{1,0:T(8,128)(2,1)}) %reduce-scatter.23.cloned.1.call-update) | async-done | bytes 262160 | tf_op jit(solution)/shard_map/reduce_scatter | solution.py:45
  666.3 14.8 %all-gather.24.cloned.1.call-done = bf16[512,1024]{1,0:T(8,128)(2,1)} async-done(((bf16[512,256]{1,0:T(8,128)(2,1)}), bf16[512,1024]{1,0:T(8,128)(2,1)}) %all-gather.24.cloned.1.call-update) | async-done | bytes 1048592 | tf_op jit(solution)/shard_map/all_gather | solution.py:41
  701.5 13.1 reduce-scatter.25.cloned.1.call-done
  741.3 9.2 pad_maximum_fusion.2
  750.5 15.7 %gather_fusion.3 = f32[192,128,128]{2,1,0:T(8,128)} fusion(f32[192,128,128]{2,1,0:T(8,128)} %pad_maximum_fusion.2, s32[1024]{0:T(1024)S(1)} %pad_clamp_fusion), kind=kCustom, calls=%fused_computation.3.clone | custom fusion | bytes 25166592 | tf_op jit(solution)/shard_map/jit(_take)/gather | solution.py:312
  802.3 9.2 pad_maximum_fusion.1
  811.5 15.4 %gather_fusion.2 = f32[192,128,128]{2,1,0:T(8,128)} fusion(f32[192,128,128]{2,1,0:T(8,128)} %pad_maximum_fusion.1, s32[1024]{0:T(1024)S(1)} %pad_clamp_fusion.1), kind=kCustom, calls=%fused_computation.1.clone | custom fusion | bytes 25166592 | tf_op jit(solution)/shard_map/jit(_take)/gather | solution.py:312
  826.9 18.2 %select_bitcast_fusion = (f32[1,192,128,128]{3,2,1,0:T(8,128)}, f32[1,192,128,128]{3,2,1,0:T(8,128)}) fusion(f32[192,128,128]{2,1,0:T(8,128)} %gather_fusion.3, pred[192]{0:T(512)(128)(4,1)S(1)} %compare_and_fusion, f32[192,128,128]{2,1,0:T(8,128)} %gather_fusion.2, pred[192]{0:T(512)(128)(4,1)S(1)} %compare_and_fusion.1), kind=kLoop, calls=%fused_computation.8 | loop fusion | flops 6291456 | bytes 50332032 | tf_op jit(solution)/shard_map/stack | solution.py:316
  845.1 9.3 pad_maximum_fusion
  854.4 8.5 copy.118
  862.9 24.7 %copy.217 = f32[24,8,256,128]{3,1,2,0:T(8,128)} copy(f32[24,8,256,128]{3,2,1,0:T(8,128)} %bitcast.332) | data formatting | bytes 50331648
  891.8 39.4 %all-reduce = (f32[2,8,256]{2,1,0:T(8,128)S(1)}, f32[2,1024]{1,0:T(2,128)S(1)}) all-reduce(f32[2,8,256]{2,1,0:T(8,128)S(1)} %pad_maximum_fusion.9, f32[2,1024]{1,0:T(2,128)S(1)} %pad_maximum_fusion.10), channel_id=1, replica_groups=mesh['dp'=8,'tensor'=4] {'dp'}, use_global_device_ids=true, to_apply=%region_64.67 | all-reduce | flops 6144 | bytes 49152 | tf_op jit(solution)/shard_map/psum | solution.py:317
  934.4 358.6 %reduce-scatter.29.cloned.1.call-done = f32[24,32768]{1,0:T(8,128)} async-done(((f32[192,32768]{1,0:T(8,128)}), f32[24,32768]{1,0:T(8,128)}) %reduce-scatter.29.cloned.1.call-update) | async-done | bytes 3145744
  1297.3 8.4 add_multiply_fusion.1
  1305.7 7.3 add_multiply_fusion
  1318.7 8.5 bitcast_subtract_fusion
  (331 shorter events, 297.7 us)
Async XLA Ops:
  7.2 1305.8 %copy-start = (f32[2,24,128,128]{3,2,1,0:T(8,128)S(1)}, f32[2,24,128,128]{3,2,1,0:T(8,128)}, u32[]{:S(2)}) copy-start(f32[2,24,128,128]{3,2,1,0:T(8,128)} %param.23) | copy-start | bytes 9437188
  7.2 182.8 %all-gather.10.cloned.1.call-start = ((), (), s32[]{:S(2)}) async-start(), calls=%async_computation.9 | async-start | bytes 14155776 | tf_op jit(solution)/shard_map/all_gather | solution.py:270
  10.7 211.0 %all-gather.12.cloned.1.call-start = ((), (), s32[]{:S(2)}) async-start(), calls=%async_computation.10 | async-start | bytes 1310720 | tf_op jit(solution)/shard_map/all_gather | solution.py:33
  12.6 248.5 %reduce-scatter.13.cloned.1.call-start = ((), (), s32[]{:S(2)}) async-start(), calls=%async_computation.11 | async-start | bytes 2621440 | tf_op jit(solution)/shard_map/reduce_scatter | solution.py:37
  12.9 212.1 %copy-start.16 = (pred[512,512]{0,1:T(8,128)(4,1)}, pred[512,512]{0,1:T(8,128)(4,1)S(1)}, u32[]{:S(2)}) copy-start(pred[512,512]{0,1:T(8,128)(4,1)S(1)} %broadcast_compare_fusion) | copy-start | bytes 786436
  231.3 46.7 %copy-start.44 = (f32[2,1024]{1,0:T(2,128)S(1)}, f32[2,1024]{1,0:T(2,128)}, u32[]{:S(2)}) copy-start(f32[2,1024]{1,0:T(2,128)} %param.25) | copy-start | bytes 24580
  231.3 64.8 %all-gather.14.cloned.1.call-start = ((), (), s32[]{:S(2)}) async-start(), calls=%async_computation.12 | async-start | bytes 1310720 | tf_op jit(solution)/shard_map/all_gather | solution.py:33
  277.8 62.4 %reduce-scatter.15.cloned.1.call-start = ((), (), s32[]{:S(2)}) async-start(), calls=%async_computation.13 | async-start | bytes 2621440 | tf_op jit(solution)/shard_map/reduce_scatter | solution.py:37
  296.1 10.0 copy-start.20
  308.6 71.9 %all-gather.16.cloned.1.call-start = ((), (), s32[]{:S(2)}) async-start(), calls=%async_computation.14 | async-start | bytes 1310720 | tf_op jit(solution)/shard_map/all_gather | solution.py:33
  357.1 71.8 %reduce-scatter.17.cloned.1.call-start = ((), (), s32[]{:S(2)}) async-start(), calls=%async_computation.15 | async-start | bytes 2621440 | tf_op jit(solution)/shard_map/reduce_scatter | solution.py:37
  396.0 68.1 %all-gather.18.cloned.1.call-start = ((), (), s32[]{:S(2)}) async-start(), calls=%async_computation.16 | async-start | bytes 1310720 | tf_op jit(solution)/shard_map/all_gather | solution.py:33
  445.8 62.5 %reduce-scatter.19.cloned.1.call-start = ((), (), s32[]{:S(2)}) async-start(), calls=%async_computation.17 | async-start | bytes 2621440 | tf_op jit(solution)/shard_map/reduce_scatter | solution.py:37
  464.1 10.0 copy-start.22
  476.7 75.4 %all-gather.20.cloned.1.call-start = ((), (), s32[]{:S(2)}) async-start(), calls=%async_computation.18 | async-start | bytes 1310720 | tf_op jit(solution)/shard_map/all_gather | solution.py:41
  534.7 51.6 %reduce-scatter.21.cloned.1.call-start = ((), (), s32[]{:S(2)}) async-start(), calls=%async_computation.19 | async-start | bytes 1310720 | tf_op jit(solution)/shard_map/reduce_scatter | solution.py:45
  552.1 6.8 copy-start.21
  561.2 53.7 %all-gather.22.cloned.1.call-start = ((), (), s32[]{:S(2)}) async-start(), calls=%async_computation.20 | async-start | bytes 1310720 | tf_op jit(solution)/shard_map/all_gather | solution.py:41
  596.8 55.6 %reduce-scatter.23.cloned.1.call-start = ((), (), s32[]{:S(2)}) async-start(), calls=%async_computation.21 | async-start | bytes 1310720 | tf_op jit(solution)/shard_map/reduce_scatter | solution.py:45
  627.4 53.6 %all-gather.24.cloned.1.call-start = ((), (), s32[]{:S(2)}) async-start(), calls=%async_computation.22 | async-start | bytes 1310720 | tf_op jit(solution)/shard_map/all_gather | solution.py:41
  662.9 51.7 %reduce-scatter.25.cloned.1.call-start = ((), (), s32[]{:S(2)}) async-start(), calls=%async_computation.23 | async-start | bytes 1310720 | tf_op jit(solution)/shard_map/reduce_scatter | solution.py:45
  681.0 6.2 copy-start.19
  689.5 88.3 %all-gather.26.cloned.1.call-start = ((), (), s32[]{:S(2)}) async-start(), calls=%async_computation.24 | async-start | bytes 1310720 | tf_op jit(solution)/shard_map/all_gather | solution.py:41
  714.6 10.7 copy-start.29
  725.2 207.2 %reduce-scatter.27.cloned.1.call-start = ((), (), s32[]{:S(2)}) async-start(), calls=%async_computation.25 | async-start | bytes 1310720 | tf_op jit(solution)/shard_map/reduce_scatter | solution.py:45
  789.6 503.4 %reduce-scatter.29.cloned.1.call-start = ((), (), s32[]{:S(2)}) async-start(), calls=%async_computation.26 | async-start | bytes 28311552
  887.8 43.5 %copy-start.45 = (f32[2,1024]{1,0:T(2,128)S(1)}, f32[2,1024]{1,0:T(2,128)}, u32[]{:S(2)}) copy-start(f32[2,1024]{1,0:T(2,128)} %param.25) | copy-start | bytes 24580
  887.8 44.1 %copy-start.43 = (f32[2,8,256]{2,1,0:T(8,128)S(1)}, f32[2,8,256]{2,1,0:T(8,128)}, u32[]{:S(2)}) copy-start(f32[2,8,256]{2,1,0:T(8,128)} %param.24) | copy-start | bytes 49156
  931.2 364.2 %copy-start.46 = (f32[2,8,256]{2,1,0:T(8,128)}, f32[2,8,256]{2,1,0:T(8,128)S(1)}, u32[]{:S(2)}) copy-start(f32[2,8,256]{2,1,0:T(8,128)S(1)} %get-tuple-element.165) | copy-start | bytes 49156
  931.2 364.2 %copy-start.49 = (f32[2,1024]{1,0:T(2,128)}, f32[2,1024]{1,0:T(2,128)S(1)}, u32[]{:S(2)}) copy-start(f32[2,1024]{1,0:T(2,128)S(1)} %get-tuple-element.166) | copy-start | bytes 24580
  1297.3 15.7 %copy-start.1 = (f32[2,24,128,128]{3,2,1,0:T(8,128)}, f32[2,24,128,128]{3,2,1,0:T(8,128)S(1)}, u32[]{:S(2)}) copy-start(f32[2,24,128,128]{3,2,1,0:T(8,128)S(1)} %copy.119) | copy-start | bytes 9437188
  1297.3 8.4 copy-start.11
  (55 other events, 140.6 us)
Sparse Core Ops, SparseCore 0:
  10.8 179.1 all-gather.9
  192.1 15.0 all-gather.11
  231.4 29.5 reduce-scatter.12
  277.9 18.1 all-gather.13
  308.8 31.3 reduce-scatter.14
  357.2 18.1 all-gather.15
  396.1 32.7 reduce-scatter.16
  445.9 18.1 all-gather.17
  476.8 31.4 reduce-scatter.18
  534.8 17.1 all-gather.19
  561.4 24.8 reduce-scatter.20
  596.9 17.9 all-gather.21
  627.5 24.8 reduce-scatter.22
  663.0 17.9 all-gather.23
  689.7 24.8 reduce-scatter.24
  725.3 17.9 all-gather.25
  789.7 25.9 reduce-scatter.26
  887.8 405.1 reduce-scatter.28
where the time goes:
time: 1350 us; the launch traced here: 1340 us
  waiting for transfers between devices  794 us (59%)
  local copies, waits for them, and re-layouts  190 us (14%)
  matrix products  120 us (9%)
  blocking collectives  109 us (8%)
  other arithmetic  107 us (8%)
  between operations  15.8 us (1%)
    unnamed x19, waiting for transfers between devices  359 us
    all_gather x1, waiting for transfers between devices, body(): lax.all_gather(masters.astype(jnp.bfloat16), 'dp', axis=1, tiled=True)  177 us
    reduce_scatter x4, waiting for transfers between devices, branch_total(): lax.psum_scatter(partial_value, 'tensor', scatter_dimension=1, tiled=True)  126 us
    unnamed x150, local copies, waits for them, and re-layouts  70 us
    reduce_scatter x4, waiting for transfers between devices, grad_total(): lax.psum_scatter(partial_value.astype(jnp.bfloat16), 'tensor', scatter_di...  62.9 us
    all_gather x4, waiting for transfers between devices, widen_grad(): lax.all_gather(values.astype(jnp.bfloat16), 'tensor', axis=1, tiled=True)  50.1 us
    psum x1, blocking collectives, body(): lax.psum((jnp.stack(vector_all), jnp.stack(up_all)), 'dp')  39.4 us
    gather x2, local copies, waits for them, and re-layouts, body(): placed = jnp.take(block_grads, inverse[layer_idx], axis=0)  31.1 us
  transfers between devices with their start and end apart: 18, of which 14 were waited for; matrix products, arithmetic and copies ran while one was open for 18% of the time, Pallas kernels for 0%

commit v1 on v0

v1 whole, which is shorter than its diff:
```python
import functools
import math

import jax
import jax.numpy as jnp
from jax import lax
from jax.experimental import pallas as pl
from jax.experimental.pallas import tpu as pltpu
from jax.sharding import PartitionSpec as P

HD = 64
eps_norm = 1e-12
stat_decay = 0.5
update_rate = 0.5
f32 = jnp.float32
bf16 = jnp.bfloat16

LAST = (((1,), (1,)), ((), ()))
FIRST = (((0,), (0,)), ((), ()))


def vmem_spec(count):
    return [pl.BlockSpec(memory_space=pltpu.VMEM)] * count


def params(mib=56):
    return pltpu.CompilerParams(vmem_limit_bytes=mib * 1024 * 1024)


def shape(dims, dtype):
    return jax.ShapeDtypeStruct(dims, dtype)


def cat_rows(refs):
    return jnp.concatenate([ref[...] for ref in refs], axis=0)


def matrix(ref, rows, cols):
    width = ref.shape[1]
    return jnp.concatenate(
        [
            jnp.concatenate(
                [ref[(r * cols + c) // width, (r * cols + c) % width] for c in range(cols)], axis=1
            )
            for r in range(rows)
        ],
        axis=0,
    )


def swap(values, axis, flip):
    count = lax.axis_size(axis)
    return lax.ppermute(values, axis, [(i, i ^ flip) for i in range(count)])


def gather_tokens(piece):
    far = swap(piece, "tensor", 2)
    near = swap(piece, "tensor", 1)
    both = swap(far, "tensor", 1)
    return (piece, far, near, both)


def scatter_sum(send, keep):
    rows = send.shape[0] // 2
    first = swap(send, "tensor", 1)
    second = swap((keep[rows:] + first[rows:].astype(f32)).astype(bf16), "tensor", 2)
    return (keep, first, second)


def to_tokens(values):
    index = lax.axis_index("tensor")
    x_pos, core = index // 2, index % 2
    rows, width = values.shape
    half, quarter = rows // 2, rows // 4
    mine = lax.dynamic_slice(values, (x_pos * half, 0), (half, width))
    other = lax.dynamic_slice(values, ((1 - x_pos) * half, 0), (half, width))
    pair = jnp.stack([mine, swap(other, "tensor", 2)])
    keep = lax.dynamic_slice(pair, (0, core * quarter, 0), (2, quarter, width))
    send = lax.dynamic_slice(pair, (0, (1 - core) * quarter, 0), (2, quarter, width))
    got = swap(send, "tensor", 1)
    relative = jnp.stack([keep[0], got[0], keep[1], got[1]])
    ordered = jnp.take(relative, jnp.arange(4) ^ index, axis=0)
    return ordered.transpose(1, 0, 2).reshape(quarter, 4 * width)


def from_tokens(values):
    index = lax.axis_index("tensor")
    rows, wide = values.shape
    width = wide // 4
    groups = values.reshape(rows, 4, width).transpose(1, 0, 2)
    relative = jnp.take(groups, jnp.arange(4) ^ index, axis=0)
    got = swap(jnp.stack([relative[1], relative[3]]), "tensor", 1)
    far = swap(jnp.stack([relative[2], got[1]]), "tensor", 2)
    chunks = jnp.stack([relative[0], got[0], far[0], far[1]])
    ordered = jnp.take(chunks, jnp.arange(4) ^ index, axis=0)
    return ordered.reshape(4 * rows, width)


def cross(values, planes):
    pairs = [(z * 2 + y, z * 2 + 1 - y) for z in planes for y in range(2)]
    return lax.ppermute(values, "dp", pairs)


def hop(values, planes, step):
    pairs = [(z * 2 + y, (z + step) * 2 + y) for z in planes for y in range(2)]
    return lax.ppermute(values, "dp", pairs)


def ends_swap(values):
    return lax.ppermute(values, "dp", [(0, 6), (1, 7), (6, 0), (7, 1)])


def after(values, *others):
    return lax.optimization_barrier((values,) + tuple(others))[0]


def spread_blocks(own):
    up_one = hop(own, (0, 1, 2), 1)
    down_one = hop(own, (1, 2, 3), -1)
    own_y = cross(own, (0, 1, 2, 3))
    up_two = hop(up_one, (1, 2), 1)
    down_two = hop(down_one, (2, 1), -1)
    ends = ends_swap(after(own, up_one, down_one))
    up_one_y = cross(up_one, (1, 2, 3))
    down_one_y = cross(down_one, (0, 1, 2))
    up_two_y = cross(up_two, (2, 3))
    down_two_y = cross(down_two, (0, 1))
    ends_y = cross(ends, (0, 3))
    return (
        (own, up_one, down_one, up_two, down_two, ends),
        (own_y, up_one_y, down_one_y, up_two_y, down_two_y, ends_y),
    )


def source_table(inverse, slots):
    dp_index = lax.axis_index("dp")
    plane, column = dp_index // 2, dp_index % 2
    end_step = 3 - 2 * plane
    steps = jnp.stack([0 * plane, plane * 0 - 1, plane * 0 + 1, plane * 0 - 2, plane * 0 + 2, end_step])
    target = plane + steps
    valid = (target >= 0) & (target <= 3)
    valid = valid.at[5].set((plane == 0) | (plane == 3))
    both_target = jnp.concatenate([target * 2 + column, target * 2 + 1 - column])
    both_valid = jnp.concatenate([valid, valid])
    picked = jnp.take(inverse.reshape(8, slots), jnp.clip(both_target, 0, 7), axis=0)
    return jnp.where(both_valid[:, None], picked, -1).astype(jnp.int32)


def assemble_kernel(source_count, slots, table, *refs):
    sources, out, sem = refs[:source_count], refs[source_count], refs[source_count + 1]
    for j in range(source_count):

        @pl.when(table[j, 0] >= 0)
        def _(j=j):
            @pl.loop(0, slots)
            def _(s):
                pltpu.make_async_copy(sources[j].at[s], out.at[table[j, s]], sem).start()

    for j in range(source_count):

        @pl.when(table[j, 0] >= 0)
        def _(j=j):
            @pl.loop(0, slots)
            def _(s):
                pltpu.make_async_copy(sources[j].at[s], out.at[table[j, s]], sem).wait()


def assemble(sources, table, total):
    slots, side = sources[0].shape[0], sources[0].shape[1]
    count = len(sources)
    return pl.pallas_call(
        functools.partial(assemble_kernel, count, slots),
        grid_spec=pltpu.PrefetchScalarGridSpec(
            num_scalar_prefetch=1,
            grid=(),
            in_specs=[pl.BlockSpec(memory_space=pl.ANY)] * count,
            out_specs=pl.BlockSpec(memory_space=pl.ANY),
            scratch_shapes=[pltpu.SemaphoreType.DMA],
        ),
        out_shape=shape((total, side, side), bf16),
        compiler_params=params(8),
        cost_estimate=pl.CostEstimate(flops=0, bytes_accessed=4 * total * side * side, transcendentals=0),
        name="assemble",
    )(table, *sources)


def gather_weights(own, owner_row):
    total = owner_row.shape[0]
    slots = own.shape[0]
    positions = jnp.arange(total, dtype=jnp.int32)
    hits = owner_row[None, :] == positions[:, None]
    inverse = jnp.sum(jnp.where(hits, positions[None, :], 0), axis=1)
    if lax.axis_size("dp") == 8:
        straight, crossed = spread_blocks(own)
        table = source_table(inverse, slots)
        last = crossed[-1]
        return assemble(straight + crossed, table, total), last
    whole = lax.all_gather(own, "dp", axis=0, tiled=True)
    return assemble((whole,), inverse[None, :].astype(jnp.int32), total), whole


def send_positions(owner_row, slots):
    if lax.axis_size("dp") != 8:
        return owner_row
    dp_index = lax.axis_index("dp")
    plane, column = dp_index // 2, dp_index % 2
    order = jnp.array([[3, 2, 1, 0], [0, 3, 2, 1], [1, 2, 3, 0], [0, 1, 2, 3]], jnp.int32)
    owner = owner_row // slots
    place = jnp.take(jnp.take(order, plane, axis=0), owner // 2)
    side = (owner % 2 == column).astype(jnp.int32)
    return ((place * 2 + side) * slots + owner_row % slots).astype(jnp.int32)


def reduce_blocks(grads, slots):
    if lax.axis_size("dp") != 8:
        return (lax.psum_scatter(grads, "dp", scatter_dimension=0, tiled=True),)
    side = grads.shape[-1]
    parts = grads.reshape(4, 2, slots, side, side)
    plane = lax.axis_index("dp") // 2
    everywhere = (0, 1, 2, 3)
    got = {}
    for k in (1, 0, 2, 3):
        got[k] = cross(parts[k, 0], everywhere)

    def total(k, *more):
        value = parts[k, 1].astype(f32) + got[k].astype(f32)
        for extra in more:
            value = value + extra.astype(f32)
        return value.astype(bf16)

    two = total(1)
    up_two = hop(two, (0, 1), 1)
    down_two = hop(two, (3, 2), -1)
    low = plane == 1
    near = total(0, jnp.where(low, down_two, up_two))
    ends = ends_swap(near)
    out_near = lax.ppermute(near, "dp", [(2, 0), (3, 1), (4, 6), (5, 7)])
    far = total(2, jnp.where(low, up_two, down_two))
    up_one = hop(far, (0, 1), 1)
    down_one = hop(far, (3, 2), -1)
    return (parts[3, 1], got[3], ends, out_near, up_one, down_one)


def norm_kernel(base, keep, first, second, vec, low_out, full_out, normed_out, scale_out, *, rows):
    bias, gain, shift = rows
    hidden = (
        base[...]
        + keep[...]
        + first[...].astype(f32)
        + second[...].astype(f32)
        + vec[bias : bias + 1, :]
    )
    center = jnp.mean(hidden, axis=1, keepdims=True)
    centred = hidden - center
    spread = jnp.mean(centred * centred, axis=1, keepdims=True)
    scale = lax.rsqrt(spread + eps_norm)
    normed = centred * scale
    full = normed * vec[gain : gain + 1, :] + vec[shift : shift + 1, :]
    full_out[...] = full
    low_out[...] = full.astype(bf16)
    normed_out[...] = normed
    scale_out[...] = scale


def top_half(array):
    return pl.BlockSpec((array.shape[0] // 2, array.shape[1]), lambda i: (0, 0))


def whole_spec(array):
    nd = len(array.shape)
    return pl.BlockSpec(tuple(array.shape), lambda i, nd=nd: (0,) * nd)


def norm_step(base, sums, vec, rows):
    keep, first, second = sums
    tokens, width = base.shape
    outs = [
        shape((tokens, width), bf16),
        shape((tokens, width), f32),
        shape((tokens, width), f32),
        shape((tokens, 1), f32),
    ]
    return pl.pallas_call(
        functools.partial(norm_kernel, rows=rows),
        grid=(1,),
        in_specs=[whole_spec(base), top_half(keep), top_half(first), whole_spec(second), whole_spec(vec)],
        out_specs=[whole_spec(o) for o in outs],
        out_shape=outs,
        compiler_params=params(24),
        cost_estimate=pl.CostEstimate(flops=20 * tokens * width, bytes_accessed=20 * tokens * width, transcendentals=tokens),
        name="norm",
    )(base, keep, first, second, vec)


def norm_back_kernel(*refs, gain, summed):
    if summed:
        base, keep, first, second, normed, scale, vec, low_out, full_out, sums_out = refs
        grad = base[...] + keep[...] + first[...].astype(f32) + second[...].astype(f32)
    else:
        base, normed, scale, vec, low_out, full_out, sums_out = refs
        grad = base[...]
    value = normed[...]
    scaled = grad * vec[gain : gain + 1, :]
    mean_grad = jnp.mean(scaled, axis=1, keepdims=True)
    mean_cross = jnp.mean(scaled * value, axis=1, keepdims=True)
    result = scale[...] * (scaled - mean_grad - value * mean_cross)
    full_out[...] = result
    low_out[...] = result.astype(bf16)
    sums_out[0:1, :] = jnp.sum(result, axis=0, keepdims=True)
    sums_out[1:2, :] = jnp.sum(grad * value, axis=0, keepdims=True)
    sums_out[2:3, :] = jnp.sum(grad, axis=0, keepdims=True)


def norm_back_step(base, sums, normed, scale, vec, gain):
    tokens, width = base.shape
    outs = [shape((tokens, width), bf16), shape((tokens, width), f32), shape((3, width), f32)]
    operands = [base]
    specs = [whole_spec(base)]
    if sums is not None:
        keep, first, second = sums
        operands += [keep, first, second]
        specs += [top_half(keep), top_half(first), whole_spec(second)]
    operands += [normed, scale, vec]
    specs += [whole_spec(normed), whole_spec(scale), whole_spec(vec)]
    return pl.pallas_call(
        functools.partial(norm_back_kernel, gain=gain, summed=sums is not None),
        grid=(1,),
        in_specs=specs,
        out_specs=[whole_spec(o) for o in outs],
        out_shape=outs,
        compiler_params=params(24),
        cost_estimate=pl.CostEstimate(flops=20 * tokens * width, bytes_accessed=20 * tokens * width, transcendentals=0),
        name="norm_back",
    )(*operands)


def store_sums(total, send_out, keep_out):
    half = total.shape[0] // 2
    send_out[...] = total[half:].astype(bf16)
    keep_out[...] = total[:half]


def attend_kernel(
    p0, p1, p2, p3, w_qkv, w_out, vec, seg_col, seg_row,
    query_out, key_out, value_out, mix_out, log_out, send_out, keep_out, bias,
):
    wide = cat_rows((p0, p1, p2, p3))
    tokens, model = wide.shape
    width = query_out.shape[1]
    tile = w_qkv.shape[-1]
    projected = jnp.dot(wide, matrix(w_qkv, model // tile, 3 * width // tile), preferred_element_type=f32)
    query = (projected[:, :width] + vec[0:1, :]).astype(bf16) * jnp.asarray(HD**-0.5, bf16)
    keys = projected[:, width : 2 * width].astype(bf16)
    values = (projected[:, 2 * width :] + vec[1:2, :]).astype(bf16)
    query_out[...] = query
    key_out[...] = keys
    value_out[...] = values
    bias[...] = jnp.where(seg_col[...] == seg_row[...], 0.0, -1e30)
    lane = lax.broadcasted_iota(jnp.int32, (tokens, 128), 1)
    logs = jnp.zeros((tokens, 128), f32)
    mixes = []
    for pair in range(width // 128):
        cols = slice(pair * 128, pair * 128 + 128)
        halves = []
        for part in range(128 // HD):
            inside = (lane >= part * HD) & (lane < part * HD + HD)
            one = jnp.where(inside, query[:, cols], jnp.zeros((), bf16))
            scores = lax.dot_general(one, keys[:, cols], LAST, preferred_element_type=f32) + bias[...]
            top = jnp.max(scores, axis=1, keepdims=True)
            exponent = jnp.exp(scores - top)
            total = jnp.sum(exponent, axis=1, keepdims=True)
            attention = (exponent * (1.0 / total)).astype(bf16)
            halves.append((inside, jnp.dot(attention, values[:, cols], preferred_element_type=f32)))
            logs = jnp.where(lane == pair * (128 // HD) + part, top + jnp.log(total), logs)
        mixed = halves[0][1]
        for inside, other in halves[1:]:
            mixed = jnp.where(inside, other, mixed)
        mixes.append(mixed.astype(bf16))
    mixture = jnp.concatenate(mixes, axis=1)
    mix_out[...] = mixture
    log_out[...] = jnp.transpose(logs)[0:8, :]
    total = jnp.dot(mixture, matrix(w_out, width // tile, model // tile), preferred_element_type=f32)
    store_sums(total, send_out, keep_out)


def block_rows(array, start, count):
    return pl.BlockSpec((count,) + tuple(array.shape[1:]), lambda i: (start // count, 0, 0, 0))


def attend_step(pieces, blocks, counts, vec, seg_col, seg_row):
    quarter, model = pieces[0].shape
    tokens, width = 4 * quarter, vec.shape[1]
    n_qkv, n_out, n_up = counts
    per = blocks.shape[1]
    outs = [
        shape((tokens, width), bf16),
        shape((tokens, width), bf16),
        shape((tokens, width), bf16),
        shape((tokens, width), bf16),
        shape((8, tokens), f32),
        shape((tokens // 2, model), bf16),
        shape((tokens // 2, model), f32),
    ]
    return pl.pallas_call(
        attend_kernel,
        grid=(1,),
        in_specs=[whole_spec(p) for p in pieces]
        + [block_rows(blocks, 0, n_qkv // per), block_rows(blocks, n_qkv // per, n_out // per)]
        + [whole_spec(vec), whole_spec(seg_col), whole_spec(seg_row)],
        out_specs=[whole_spec(o) for o in outs],
        out_shape=outs,
        scratch_shapes=[pltpu.VMEM((tokens, tokens), f32)],
        compiler_params=params(),
        cost_estimate=pl.CostEstimate(
            flops=2 * tokens * model * 4 * width + 4 * tokens * tokens * width * 2,
            bytes_accessed=8 * 1024 * 1024,
            transcendentals=tokens * tokens * width // HD,
        ),
        name="attend",
    )(*pieces, blocks, blocks, vec, seg_col, seg_row)


def attend_back_kernel(
    p0, p1, p2, p3, w_out, w_qkv, query_in, key_in, value_in, log_in, seg_col, seg_row,
    grad_out, sums_out, send_out, keep_out, bias,
):
    wide = cat_rows((p0, p1, p2, p3))
    tokens, model = wide.shape
    width = query_in.shape[1]
    tile = w_qkv.shape[-1]
    grad_mix = lax.dot_general(
        wide, matrix(w_out, width // tile, model // tile), LAST, preferred_element_type=f32
    ).astype(bf16)
    bias[...] = jnp.where(seg_col[...] == seg_row[...], 0.0, -1e30)
    lane = lax.broadcasted_iota(jnp.int32, (tokens, 128), 1)
    grads = ([], [], [])
    for pair in range(width // 128):
        cols = slice(pair * 128, pair * 128 + 128)
        query, keys, values, mix = query_in[:, cols], key_in[:, cols], value_in[:, cols], grad_mix[:, cols]
        picked = [None, None, None]
        for part in range(128 // HD):
            head = pair * (128 // HD) + part
            inside = (lane >= part * HD) & (lane < part * HD + HD)
            zero = jnp.zeros((), bf16)
            scores = (
                lax.dot_general(jnp.where(inside, keys, zero), query, LAST, preferred_element_type=f32)
                + bias[...]
            )
            attention = jnp.exp(scores - log_in[head : head + 1, :])
            pulled = lax.dot_general(jnp.where(inside, values, zero), mix, LAST, preferred_element_type=f32)
            inner = jnp.sum(attention * pulled, axis=0, keepdims=True)
            grad_scores = (attention * (pulled - inner)).astype(bf16)
            three = (
                lax.dot_general(grad_scores, keys, FIRST, preferred_element_type=f32) * (HD**-0.5),
                jnp.dot(grad_scores, query, preferred_element_type=f32),
                jnp.dot(attention.astype(bf16), mix, preferred_element_type=f32),
            )
            for which in range(3):
                if part == 0:
                    picked[which] = three[which]
                else:
                    picked[which] = jnp.where(inside, three[which], picked[which])
        for which in range(3):
            grads[which].append(picked[which].astype(bf16))
    joined = [jnp.concatenate(g, axis=1) for g in grads]
    every = jnp.concatenate(joined, axis=1)
    grad_out[...] = every
    sums_out[0:1, :] = jnp.sum(joined[0].astype(f32), axis=0, keepdims=True)
    sums_out[1:2, :] = jnp.sum(joined[2].astype(f32), axis=0, keepdims=True)
    total = lax.dot_general(
        every, matrix(w_qkv, model // tile, 3 * width // tile), LAST, preferred_element_type=f32
    )
    store_sums(total, send_out, keep_out)


def attend_back_step(pieces, blocks, counts, query, keys, values, logs, seg_col, seg_row):
    quarter, model = pieces[0].shape
    tokens, width = query.shape
    n_qkv, n_out, n_up = counts
    per = blocks.shape[1]
    outs = [
        shape((tokens, 3 * width), bf16),
        shape((2, width), f32),
        shape((tokens // 2, model), bf16),
        shape((tokens // 2, model), f32),
    ]
    return pl.pallas_call(
        attend_back_kernel,
        grid=(1,),
        in_specs=[whole_spec(p) for p in pieces]
        + [block_rows(blocks, n_qkv // per, n_out // per), block_rows(blocks, 0, n_qkv // per)]
        + [whole_spec(a) for a in (query, keys, values, logs, seg_col, seg_row)],
        out_specs=[whole_spec(o) for o in outs],
        out_shape=outs,
        scratch_shapes=[pltpu.VMEM((tokens, tokens), f32)],
        compiler_params=params(),
        cost_estimate=pl.CostEstimate(
            flops=2 * tokens * model * 4 * width + 10 * tokens * tokens * width * 2,
            bytes_accessed=8 * 1024 * 1024,
            transcendentals=tokens * tokens * width // HD,
        ),
        name="attend_back",
    )(*pieces, blocks, blocks, query, keys, values, logs, seg_col, seg_row)


def ffn_kernel(p0, p1, p2, p3, w_up, w_down, bias, act_out, slope_out, send_out, keep_out, total):
    step = pl.program_id(0)
    wide = cat_rows((p0, p1, p2, p3))
    model = wide.shape[1]
    tile = w_up.shape[-1]
    cols = act_out.shape[1] // tile
    pre = jnp.dot(wide, matrix(w_up, model // tile, cols), preferred_element_type=f32) + bias[...]
    cdf = 0.5 + 0.5 * lax.erf(pre * (0.5**0.5))
    slope_out[...] = cdf + pre * (jnp.exp(-0.5 * pre * pre) * (1.0 / math.sqrt(2.0 * math.pi)))
    activated = (pre * cdf).astype(bf16)
    act_out[...] = activated
    part = jnp.dot(activated, matrix(w_down, cols, model // tile), preferred_element_type=f32)

    @pl.when(step == 0)
    def _():
        total[...] = part

    @pl.when(step > 0)
    def _():
        total[...] += part

    @pl.when(step == pl.num_programs(0) - 1)
    def _():
        store_sums(total[...], send_out, keep_out)


def fixed(array):
    nd = len(array.shape)
    return pl.BlockSpec(tuple(array.shape), lambda i, nd=nd: (0,) * nd)


def ffn_specs(blocks, counts, chunk_blocks):
    n_qkv, n_out, n_up = counts
    per = blocks.shape[1]
    side = blocks.shape[2]
    up_row = (n_qkv + n_out) // per
    up_rows = n_up // per
    down_row = (n_qkv + n_out + n_up) // per
    up_spec = pl.BlockSpec((up_rows, chunk_blocks, side, side), lambda i: (up_row // up_rows, i, 0, 0))
    down_spec = pl.BlockSpec((chunk_blocks, per, side, side), lambda i: (down_row // chunk_blocks + i, 0, 0, 0))
    return up_spec, down_spec


def ffn_step(pieces, blocks, counts, up_bias, steps=4):
    quarter, model = pieces[0].shape
    tokens, hidden = 4 * quarter, up_bias.shape[1]
    chunk = hidden // steps
    up_spec, down_spec = ffn_specs(blocks, counts, chunk // blocks.shape[2])
    outs = [
        shape((tokens, hidden), bf16),
        shape((tokens, hidden), f32),
        shape((tokens // 2, model), bf16),
        shape((tokens // 2, model), f32),
    ]
    by_cols = pl.BlockSpec((tokens, chunk), lambda i: (0, i))
    return pl.pallas_call(
        ffn_kernel,
        grid=(steps,),
        in_specs=[fixed(p) for p in pieces]
        + [up_spec, down_spec, pl.BlockSpec((1, chunk), lambda i: (0, i))],
        out_specs=[by_cols, by_cols, fixed(outs[2]), fixed(outs[3])],
        out_shape=outs,
        scratch_shapes=[pltpu.VMEM((tokens, model), f32)],
        compiler_params=params(),
        cost_estimate=pl.CostEstimate(
            flops=4 * tokens * model * hidden, bytes_accessed=10 * 1024 * 1024, transcendentals=2 * tokens * hidden
        ),
        name="ffn",
    )(*pieces, blocks, blocks, up_bias)


def ffn_back_kernel(p0, p1, p2, p3, w_up, w_down, slope, grad_out, bias_out, send_out, keep_out, total):
    step = pl.program_id(0)
    wide = cat_rows((p0, p1, p2, p3))
    model = wide.shape[1]
    tile = w_up.shape[-1]
    cols = grad_out.shape[1] // tile
    pulled = lax.dot_general(wide, matrix(w_down, cols, model // tile), LAST, preferred_element_type=f32)
    grad = (pulled * slope[...]).astype(bf16)
    grad_out[...] = grad
    bias_out[...] = jnp.sum(grad.astype(f32), axis=0, keepdims=True)
    part = lax.dot_general(grad, matrix(w_up, model // tile, cols), LAST, preferred_element_type=f32)

    @pl.when(step == 0)
    def _():
        total[...] = part

    @pl.when(step > 0)
    def _():
        total[...] += part

    @pl.when(step == pl.num_programs(0) - 1)
    def _():
        store_sums(total[...], send_out, keep_out)


def ffn_back_step(pieces, blocks, counts, slope, steps=4):
    quarter, model = pieces[0].shape
    tokens, hidden = slope.shape
    chunk = hidden // steps
    up_spec, down_spec = ffn_specs(blocks, counts, chunk // blocks.shape[2])
    outs = [
        shape((tokens, hidden), bf16),
        shape((1, hidden), f32),
        shape((tokens // 2, model), bf16),
        shape((tokens // 2, model), f32),
    ]
    by_cols = pl.BlockSpec((tokens, chunk), lambda i: (0, i))
    return pl.pallas_call(
        ffn_back_kernel,
        grid=(steps,),
        in_specs=[fixed(p) for p in pieces] + [up_spec, down_spec, by_cols],
        out_specs=[by_cols, pl.BlockSpec((1, chunk), lambda i: (0, i)), fixed(outs[2]), fixed(outs[3])],
        out_shape=outs,
        scratch_shapes=[pltpu.VMEM((tokens, model), f32)],
        compiler_params=params(),
        cost_estimate=pl.CostEstimate(
            flops=4 * tokens * model * hidden, bytes_accessed=10 * 1024 * 1024, transcendentals=0
        ),
        name="ffn_back",
    )(*pieces, blocks, blocks, slope)


def weight_grad_kernel(jobs, chained, place, *refs):
    counts = [count for job in jobs for count in job[:2]]
    used = sum(counts)
    operands, rest = refs[:used], refs[used + chained :]
    out, stage, sem = rest
    side = stage.shape[-1]
    at = 0
    done = []
    slot = 0
    for left_count, right_count, base in jobs:
        left = operands[at : at + left_count]
        right = operands[at + left_count : at + left_count + right_count]
        at += left_count + right_count
        columns = cat_rows(right)
        per = columns.shape[1] // side
        width = left[0].shape[1]
        chunk = min(width, 2 * side)
        for start in range(0, width, chunk):
            rows = jnp.concatenate([ref[:, start : start + chunk] for ref in left], axis=0)
            result = lax.dot_general(rows, columns, FIRST, preferred_element_type=f32).astype(bf16)
            for i in range(chunk // side):
                for j in range(per):
                    block = base + (start // side + i) * per + j
                    stage[slot] = result[i * side : (i + 1) * side, j * side : (j + 1) * side]
                    pltpu.make_async_copy(stage.at[slot], out.at[place[block]], sem).start()
                    done.append((slot, block))
                    slot += 1
    for slot, block in done:
        pltpu.make_async_copy(stage.at[slot], out.at[place[block]], sem).wait()


def weight_grad_step(jobs, place, target, total, side):
    operands = [a for left, right, base in jobs for a in left + right]
    layout = tuple((len(left), len(right), base) for left, right, base in jobs)
    blocks = sum(
        left[0].shape[1] // side * (right[0].shape[1] // side) for left, right, base in jobs
    )
    chained = 0 if target is None else 1
    extra = [] if target is None else [target]
    aliases = {} if target is None else {1 + len(operands): 0}
    tokens = sum(a.shape[0] for a in jobs[0][0])
    return pl.pallas_call(
        functools.partial(weight_grad_kernel, layout, chained),
        grid_spec=pltpu.PrefetchScalarGridSpec(
            num_scalar_prefetch=1,
            grid=(),
            in_specs=vmem_spec(len(operands)) + [pl.BlockSpec(memory_space=pl.ANY)] * chained,
            out_specs=pl.BlockSpec(memory_space=pl.ANY),
            scratch_shapes=[pltpu.VMEM((blocks, side, side), bf16), pltpu.SemaphoreType.DMA],
        ),
        out_shape=shape((total, side, side), bf16),
        input_output_aliases=aliases,
        compiler_params=params(),
        cost_estimate=pl.CostEstimate(
            flops=2 * tokens * blocks * side * side,
            bytes_accessed=4 * blocks * side * side,
            transcendentals=0,
        ),
        name="weight_grad",
    )(place, *operands, *extra)


def update_kernel(part_count, chained, *refs):
    parts = refs[:part_count]
    masters, left, right, left_root, right_root = refs[part_count : part_count + 5]
    grad_out, left_out, right_out, weight_out = refs[part_count + 5 + chained :]
    grad = parts[0][...].astype(f32)
    for part in parts[1:]:
        grad = grad + part[...].astype(f32)
    grad_out[0] = grad
    for b in range(grad.shape[0]):
        low = grad[b].astype(bf16)
        left_out[0, b] = stat_decay * left[0, b] + (1.0 - stat_decay) * lax.dot_general(
            low, low, LAST, preferred_element_type=f32
        )
        right_out[0, b] = stat_decay * right[0, b] + (1.0 - stat_decay) * lax.dot_general(
            low, low, FIRST, preferred_element_type=f32
        )
        inner = jnp.dot(low, right_root[0, b].astype(bf16), preferred_element_type=f32)
        outer = jnp.dot(left_root[0, b].astype(bf16), inner.astype(bf16), preferred_element_type=f32)
        weight_out[0, b] = masters[0, b] - update_rate * outer


def update_step(parts, layer, state, previous):
    layers, slots, side, _ = state[0].shape
    group = 4 if slots % 4 == 0 else slots
    one = pl.BlockSpec((1, group, side, side), lambda i: (layer, i, 0, 0))
    chained = [] if previous is None else list(previous)
    aliases = {len(parts) + 5 + k: k for k in range(len(chained))}
    return pl.pallas_call(
        functools.partial(update_kernel, len(parts), len(chained)),
        grid=(slots // group,),
        in_specs=[pl.BlockSpec((group, side, side), lambda i: (i, 0, 0))] * len(parts)
        + [one] * 5
        + [pl.BlockSpec(memory_space=pl.ANY)] * len(chained),
        out_specs=[one] * 4,
        out_shape=[shape(state[0].shape, f32)] * 4,
        input_output_aliases=aliases,
        compiler_params=params(32),
        cost_estimate=pl.CostEstimate(
            flops=8 * slots * side**3, bytes_accessed=44 * slots * side * side, transcendentals=0
        ),
        name="update",
    )(*parts, *state, *chained)


def sum_all(values):
    if lax.axis_size("dp") != 8:
        return lax.psum(values, ("dp", "tensor"))
    values = values + swap(values, "tensor", 1)
    values = values + swap(values, "tensor", 2)
    values = values + swap(values, "dp", 1)
    values = values + swap(values, "dp", 2)
    return values + swap(values, "dp", 4)


def body(
    layer_in,
    cotangent,
    segment_ids,
    owner_map,
    masters,
    left_stats,
    right_stats,
    left_roots,
    right_roots,
    vectors,
    up_bias,
):
    layers, slots, side = masters.shape[0], masters.shape[1], masters.shape[-1]
    tokens, width = layer_in.shape
    model = width * lax.axis_size("tensor")
    hidden = up_bias.shape[1]
    tile_rows = model // side
    n_qkv = tile_rows * (3 * width // side)
    n_out = width // side * tile_rows
    n_up = tile_rows * (hidden // side)
    counts = (n_qkv, n_out, n_up)
    total = owner_map.shape[1]
    index = lax.axis_index("tensor")
    quarter = tokens // 4

    low = [masters[layer].astype(bf16) for layer in range(layers)]
    weights = []
    last = None
    for layer in range(layers):
        own = low[layer] if last is None else after(low[layer], last)
        gathered, last = gather_weights(own, owner_map[layer])
        weights.append(gathered.reshape(total // tile_rows, tile_rows, side, side))

    order = jnp.array([0, 2, 1, 3]) ^ index
    segments = jnp.take(segment_ids.reshape(4, quarter), order, axis=0).reshape(tokens)
    seg_col, seg_row = segments[:, None], segments[None, :]
    wide_vectors = lax.all_gather(vectors, "tensor", axis=2, tiled=True)

    stream = to_tokens(layer_in)
    stream_low = stream.astype(bf16)
    grad = to_tokens(cotangent)

    kept = []
    for layer in range(layers):
        vec, blocks = wide_vectors[layer], weights[layer]
        wide_in = gather_tokens(stream_low)
        query, keys, values, mixture, logs, send, keep = attend_step(
            wide_in, blocks, counts, vectors[layer], seg_col, seg_row
        )
        mid_low, middle, normed_one, scale_one = norm_step(stream, scatter_sum(send, keep), vec, (2, 3, 4))
        wide_mid = gather_tokens(mid_low)
        activated, slope, send, keep = ffn_step(wide_mid, blocks, counts, up_bias[layer : layer + 1])
        stream_low, stream, normed_two, scale_two = norm_step(middle, scatter_sum(send, keep), vec, (5, 6, 7))
        kept.append(
            (wide_in, query, keys, values, mixture, logs, normed_one, scale_one, wide_mid, activated, slope, normed_two, scale_two)
        )
    layer_out = from_tokens(stream)

    vector_sums = [None] * layers
    bias_sums = [None] * layers
    state = (masters, left_stats, right_stats, left_roots, right_roots)
    updated = None
    sums = None
    for layer in reversed(range(layers)):
        vec, blocks = wide_vectors[layer], weights[layer]
        (wide_in, query, keys, values, mixture, logs, normed_one, scale_one, wide_mid, activated, slope, normed_two, scale_two) = kept[layer]
        place = send_positions(owner_map[layer], slots)
        grad_low, grad_two, sums_two = norm_back_step(grad, sums, normed_two, scale_two, vec, 6)
        wide_grad = gather_tokens(grad_low)
        grad_pre, bias_sum, send, keep = ffn_back_step(wide_grad, blocks, counts, slope)
        sums = scatter_sum(send, keep)
        block_grads = weight_grad_step(
            [((wide_mid), (grad_pre,), n_qkv + n_out), ((activated,), (wide_grad), n_qkv + n_out + n_up)],
            place, None, total, side,
        )
        grad_low, grad_one, sums_one = norm_back_step(grad_two, sums, normed_one, scale_one, vec, 3)
        wide_first = gather_tokens(grad_low)
        grad_qkv, qv_sums, send, keep = attend_back_step(
            wide_first, blocks, counts, query, keys, values, logs, seg_col, seg_row
        )
        sums = scatter_sum(send, keep)
        block_grads = weight_grad_step(
            [((wide_in), (grad_qkv,), 0), ((mixture,), (wide_first), n_qkv)],
            place, block_grads, total, side,
        )
        grad = grad_one
        parts = reduce_blocks(block_grads, slots)
        updated = update_step(parts, layer, state, updated)
        spread = jnp.concatenate([jnp.zeros_like(sums_one[:2]), sums_one, sums_two], axis=0)
        vector_sums[layer] = lax.dynamic_update_slice(spread, qv_sums, (0, index * width))
        bias_sums[layer] = lax.dynamic_update_slice(
            jnp.zeros((1, 4 * hidden), f32), bias_sum, (0, index * hidden)
        ).reshape(4 * hidden // model, model)
    input_grad = from_tokens(
        grad + sums[0][:quarter] + sums[1][:quarter].astype(f32) + sums[2].astype(f32)
    )

    small = sum_all(jnp.stack([jnp.concatenate(pair, axis=0) for pair in zip(vector_sums, bias_sums)]))
    vector_grads = lax.dynamic_slice(small[:, :8], (0, 0, index * width), (layers, 8, width))
    up_bias_grads = lax.dynamic_slice(
        small[:, 8:].reshape(layers, 4 * hidden), (0, index * hidden), (layers, hidden)
    )
    reduced, left_new, right_new, new_weights = updated
    vector_rate = 0.5 / math.sqrt(tokens * lax.axis_size("dp"))
    return (
        layer_out,
        input_grad,
        reduced,
        left_new,
        right_new,
        new_weights,
        vector_grads,
        vectors - vector_rate * vector_grads,
        up_bias_grads,
        up_bias - vector_rate * up_bias_grads,
    )


def solution(mesh):
    owned = P(None, ("dp", "tensor"), None, None)
    return jax.shard_map(
        body,
        mesh=mesh,
        in_specs=(
            P("dp", "tensor"),
            P("dp", "tensor"),
            P("dp", None),
            P(),
            owned,
            owned,
            owned,
            owned,
            owned,
            P(None, None, "tensor"),
            P(None, "tensor"),
        ),
        out_specs=(
            P("dp", "tensor"),
            P("dp", "tensor"),
            owned,
            owned,
            owned,
            owned,
            P(None, None, "tensor"),
            P(None, None, "tensor"),
            P(None, "tensor"),
            P(None, "tensor"),
        ),
        check_vma=False,
    )
```

time: 1350 us -> 642 us (0.48)
  waiting for transfers between devices: 794 us -> 280 us
  Pallas kernels: 0 us -> 125 us
  local copies, waits for them, and re-layouts: 190 us -> 65.1 us
  matrix products: 120 us -> 0 us
  starting transfers between devices: 1.92 us -> 106 us
  blocking collectives: 109 us -> 6.7 us
  other arithmetic: 107 us -> 45.8 us
    unnamed x19 -> x0, waiting for transfers between devices: 359 us -> none
    ppermute x0 -> x95, waiting for transfers between devices: none -> 280 us  [the longest x53 127 us: swap(): return lax.ppermute(values, axis, [(i, i ^ flip) for i in range(count)])]
    all_gather x9 -> x0, waiting for transfers between devices: 247 us -> none  [the longest x1 177 us: body(): lax.all_gather(masters.astype(jnp.bfloat16), 'dp', axis=1, tiled=True)]
    reduce_scatter x8 -> x0, waiting for transfers between devices: 189 us -> none  [the longest x4 126 us: branch_total(): lax.psum_scatter(partial_value, 'tensor', scatter_dimension=1, tiled=True)]
    pallas_call x0 -> x24, Pallas kernels: none -> 125 us  [the longest x4 21.3 us: weight_grad_step(): pl.pallas_call(functools.partial(weight_grad_kernel, layout, chained), gr...]
    dot_general x40 -> x0, matrix products: 120 us -> none  [the longest x2 18 us: forward_layer(): jnp.dot(wide_mid, up_weight, preferred_element_type=jnp.float32) + up_row]
    psum x13 -> x0, blocking collectives: 109 us -> none  [the longest x1 39.4 us: body(): lax.psum((jnp.stack(vector_all), jnp.stack(up_all)), 'dp')]
    ppermute x0 -> x95, starting transfers between devices: none -> 106 us  [the longest x20 30.5 us: cross(): return lax.ppermute(values, 'dp', pairs)]
  transfers between devices with their start and end apart: 18 -> 95, of which waited for: 14 -> 41; matrix products, arithmetic and copies ran while one was open for 18% -> 10% of each run, Pallas kernels for 0% -> 10%
where the time goes in v1:
time: 642 us; the launch traced here: 631 us
  waiting for transfers between devices  280 us (44%)
  Pallas kernels  125 us (19%)
  starting transfers between devices  106 us (17%)
  local copies, waits for them, and re-layouts  65.1 us (10%)
  other arithmetic  45.8 us (7%)
  blocking collectives  6.7 us (1%)
    ppermute x53, waiting for transfers between devices, swap(): return lax.ppermute(values, axis, [(i, i ^ flip) for i in range(count)])  127 us
    ppermute x20, waiting for transfers between devices, cross(): return lax.ppermute(values, 'dp', pairs)  72.7 us
    ppermute x16, waiting for transfers between devices, hop(): return lax.ppermute(values, 'dp', pairs)  48.4 us
    unnamed x180, local copies, waits for them, and re-layouts  37.4 us
    ppermute x20, starting transfers between devices, cross(): return lax.ppermute(values, 'dp', pairs)  30.5 us
    ppermute x16, starting transfers between devices, hop(): return lax.ppermute(values, 'dp', pairs)  30 us
    ppermute x2, waiting for transfers between devices, reduce_blocks(): out_near = lax.ppermute(near, 'dp', [(2, 0), (3, 1), (4, 6), (5, 7)])  24.9 us
    ppermute x53, starting transfers between devices, swap(): return lax.ppermute(values, axis, [(i, i ^ flip) for i in range(count)])  24.8 us
  transfers between devices with their start and end apart: 95, of which 41 were waited for; matrix products, arithmetic and copies ran while one was open for 10% of the time, Pallas kernels for 10%

profile of v1, /device:TPU:0, one launch (start us, length us, event | category | flops | bytes accessed | tf_op | source)
XLA Modules:
  0.0 631.0 jit_solution(17995122068839283796)
XLA Ops:
  31.5 7.1 %collective-permute-start.9 = (bf16[24,128,128]{2,1,0:T(8,128)(2,1)S(1)}, bf16[24,128,128]{2,1,0:T(8,128)(2,1)}, u32[]{:S(2)}, u32[]{:S(2)}) collective-permute-start(bf16[24,128,128]{2,1,0:T(8,128)(2,1)S(1)} %get-tuple-element.110.refs_0_), channel_id=1, source_target_pairs={{0,24},{4,28},{24,0},{28,4},{1,25},{5,29},{25,1},{29,5},{2,26},{6,... | collective-permute-start | bytes 2359304 | tf_op jit(solution)/shard_map/ppermute | solution.py:110
  55.8 17.7 %collective-permute-done.8.refs_4_ = bf16[24,128,128]{2,1,0:T(8,128)(2,1)} collective-permute-done((bf16[24,128,128]{2,1,0:T(8,128)(2,1)}, bf16[24,128,128]{2,1,0:T(8,128)(2,1)}, u32[]{:S(2)}, u32[]{:S(2)}) %collective-permute-start.8) | collective-permute-done | bytes 786464 | tf_op jit(solution)/shard_map/ppermute | solution.py:106
  84.5 11.5 %collective-permute-done.14.refs_10_ = bf16[24,128,128]{2,1,0:T(8,128)(2,1)} collective-permute-done((bf16[24,128,128]{2,1,0:T(8,128)(2,1)}, bf16[24,128,128]{2,1,0:T(8,128)(2,1)}, u32[]{:S(2)}, u32[]{:S(2)}) %collective-permute-start.14) | collective-permute-done | bytes 786464 | tf_op jit(solution)/shard_map/ppermute | solution.py:101
  96.1 15.9 %collective-permute-done.15.refs_11_ = bf16[24,128,128]{2,1,0:T(8,128)(2,1)} collective-permute-done((bf16[24,128,128]{2,1,0:T(8,128)(2,1)}, bf16[24,128,128]{2,1,0:T(8,128)(2,1)}, u32[]{:S(2)}, u32[]{:S(2)}) %collective-permute-start.15) | collective-permute-done | bytes 786464 | tf_op jit(solution)/shard_map/ppermute | solution.py:101
  135.2 6.7 %all_gather.3 = f32[2,8,1024]{2,1,0:T(8,128)S(1)} all-gather(f32[2,8,256]{2,1,0:T(8,128)S(1)} %copy-done.73), channel_id=1, replica_groups=mesh['dp'=8,'tensor'=4] {'tensor'}, dimensions={2}, use_global_device_ids=true | all-gather | bytes 81920 | tf_op jit(solution)/shard_map/all_gather | solution.py:782
  154.3 9.3 %ffn.2 = (bf16[512,1024]{1,0:T(8,128)(2,1)}, f32[512,1024]{1,0:T(8,128)}, bf16[256,1024]{1,0:T(8,128)(2,1)}, f32[256,1024]{1,0:T(8,128)}) custom-call(bf16[128,1024]{1,0:T(8,128)(2,1)} %copy-done.27, bf16[128,1024]{1,0:T(8,128)(2,1)} %copy-done.61, bf16[128,1024]{1,0:T(8,128)(2,1)} %copy-done.62, bf16[128,1024]{1,0:T(8,128)(2,1)} %copy-done.63, ...), custom_call_target="tpu_custom_call" | custom-call | flops 2147483648 | bytes 10485760 | tf_op jit(solution)/shard_map/ffn/pallas_call | solution.py:561
  167.2 6.8 %collective-permute-start.30 = (bf16[24,128,128]{2,1,0:T(8,128)(2,1)S(1)}, bf16[24,128,128]{2,1,0:T(8,128)(2,1)S(1)}, u32[]{:S(2)}, u32[]{:S(2)}) collective-permute-start(bf16[24,128,128]{2,1,0:T(8,128)(2,1)S(1)} %get-tuple-element.120.refs_0_), channel_id=1, source_target_pairs={{0,24},{4,28},{24,0},{28,4},{1,25},{5,29},{25,1},{29,5},{2,26},{6,... | collective-permute-start | bytes 2359304 | tf_op jit(solution)/shard_map/ppermute | solution.py:110
  178.8 28.6 %collective-permute-done.29.refs_4_ = bf16[24,128,128]{2,1,0:T(8,128)(2,1)S(1)} collective-permute-done((bf16[24,128,128]{2,1,0:T(8,128)(2,1)S(1)}, bf16[24,128,128]{2,1,0:T(8,128)(2,1)S(1)}, u32[]{:S(2)}, u32[]{:S(2)}) %collective-permute-start.29) | collective-permute-done | bytes 786464 | tf_op jit(solution)/shard_map/ppermute | solution.py:106
  215.4 6.9 %collective-permute-done.23.p1.refs_1_ = bf16[128,1024]{1,0:T(8,128)(2,1)S(1)} collective-permute-done((bf16[128,1024]{1,0:T(8,128)(2,1)S(1)}, bf16[128,1024]{1,0:T(8,128)(2,1)S(1)}, u32[]{:S(2)}, u32[]{:S(2)}) %collective-permute-start.23) | collective-permute-done | bytes 262176 | tf_op jit(solution)/shard_map/ppermute | solution.py:53
  222.3 8.2 %collective-permute-done.35.refs_10_ = bf16[24,128,128]{2,1,0:T(8,128)(2,1)S(1)} collective-permute-done((bf16[24,128,128]{2,1,0:T(8,128)(2,1)S(1)}, bf16[24,128,128]{2,1,0:T(8,128)(2,1)S(1)}, u32[]{:S(2)}, u32[]{:S(2)}) %collective-permute-start.35) | collective-permute-done | bytes 786464 | tf_op jit(solution)/shard_map/ppermute | solution.py:101
  230.5 15.6 %collective-permute-done.36.refs_11_ = bf16[24,128,128]{2,1,0:T(8,128)(2,1)S(1)} collective-permute-done((bf16[24,128,128]{2,1,0:T(8,128)(2,1)S(1)}, bf16[24,128,128]{2,1,0:T(8,128)(2,1)S(1)}, u32[]{:S(2)}, u32[]{:S(2)}) %collective-permute-start.36) | collective-permute-done | bytes 786464 | tf_op jit(solution)/shard_map/ppermute | solution.py:101
  246.1 12.0 %assemble.3 = bf16[192,128,128]{2,1,0:T(8,128)(2,1)S(1)} custom-call(s32[12,24]{1,0:T(8,128)S(1)} %get-tuple-element.257.table, bf16[24,128,128]{2,1,0:T(8,128)(2,1)S(1)} %get-tuple-element.120.refs_0_, bf16[24,128,128]{2,1,0:T(8,128)(2,1)S(1)} %collective-permute-done.26.refs_1_, bf16[24,128,128]{2,1,0:T(8,128)(2,1)S(1)} %collective-permute-done.27.refs_2_, ...), custom_call_target="tpu_custom_call" | custom-call | bytes 12582912 | tf_op jit(solution)/shard_map/assemble/pallas_call | solution.py:171
  272.0 7.8 %collective-permute-done.38.second = bf16[128,1024]{1,0:T(8,128)(2,1)S(1)} collective-permute-done((bf16[128,1024]{1,0:T(8,128)(2,1)S(1)}, bf16[128,1024]{1,0:T(8,128)(2,1)S(1)}, u32[]{:S(2)}, u32[]{:S(2)}) %collective-permute-start.38) | collective-permute-done | bytes 262176 | tf_op jit(solution)/shard_map/ppermute | solution.py:53
  280.8 7.0 %collective-permute-done.39.p1.refs_1_ = bf16[128,1024]{1,0:T(8,128)(2,1)S(1)} collective-permute-done((bf16[128,1024]{1,0:T(8,128)(2,1)S(1)}, bf16[128,1024]{1,0:T(8,128)(2,1)S(1)}, u32[]{:S(2)}, u32[]{:S(2)}) %collective-permute-start.39) | collective-permute-done | bytes 262176 | tf_op jit(solution)/shard_map/ppermute | solution.py:53
  290.0 9.4 %ffn.3 = (bf16[512,1024]{1,0:T(8,128)(2,1)}, f32[512,1024]{1,0:T(8,128)}, bf16[256,1024]{1,0:T(8,128)(2,1)}, f32[256,1024]{1,0:T(8,128)}) custom-call(bf16[128,1024]{1,0:T(8,128)(2,1)} %copy-done.28, bf16[128,1024]{1,0:T(8,128)(2,1)} %copy-done.64, bf16[128,1024]{1,0:T(8,128)(2,1)} %copy-done.65, bf16[128,1024]{1,0:T(8,128)(2,1)} %copy-done.66, ...), custom_call_target="tpu_custom_call" | custom-call | flops 2147483648 | bytes 10485760 | tf_op jit(solution)/shard_map/ffn/pallas_call | solution.py:561
  303.4 7.8 %collective-permute-done.43.second = bf16[128,1024]{1,0:T(8,128)(2,1)S(1)} collective-permute-done((bf16[128,1024]{1,0:T(8,128)(2,1)S(1)}, bf16[128,1024]{1,0:T(8,128)(2,1)S(1)}, u32[]{:S(2)}, u32[]{:S(2)}) %collective-permute-start.43) | collective-permute-done | bytes 262176 | tf_op jit(solution)/shard_map/ppermute | solution.py:53
  313.1 7.0 %collective-permute-done.48.p1.refs_7_ = bf16[128,1024]{1,0:T(8,128)(2,1)S(1)} collective-permute-done((bf16[128,1024]{1,0:T(8,128)(2,1)S(1)}, bf16[128,1024]{1,0:T(8,128)(2,1)S(1)}, u32[]{:S(2)}, u32[]{:S(2)}) %collective-permute-start.48) | collective-permute-done | bytes 262176 | tf_op jit(solution)/shard_map/ppermute | solution.py:53
  322.3 9.2 %ffn_back.2 = (bf16[512,1024]{1,0:T(8,128)(2,1)}, f32[1,1024]{1,0:T(1,128)}, bf16[256,1024]{1,0:T(8,128)(2,1)}, f32[256,1024]{1,0:T(8,128)}) custom-call(bf16[128,1024]{1,0:T(8,128)(2,1)} %copy-done.26, bf16[128,1024]{1,0:T(8,128)(2,1)} %copy-done.58, bf16[128,1024]{1,0:T(8,128)(2,1)} %copy-done.59, bf16[128,1024]{1,0:T(8,128)(2,1)} %copy-done.60, ...), custom_call_target="tpu_custom_call" | custom-call | flops 2147483648 | bytes 10485760 | tf_op jit(solution)/shard_map/ffn_back/pallas_call | solution.py:614
  335.4 7.8 %collective-permute-done.52.refs_3_ = bf16[128,1024]{1,0:T(8,128)(2,1)S(1)} collective-permute-done((bf16[128,1024]{1,0:T(8,128)(2,1)S(1)}, bf16[128,1024]{1,0:T(8,128)(2,1)S(1)}, u32[]{:S(2)}, u32[]{:S(2)}) %collective-permute-start.52) | collective-permute-done | bytes 262176 | tf_op jit(solution)/shard_map/ppermute | solution.py:53
  345.0 7.0 %collective-permute-done.53.p1.refs_7_ = bf16[128,1024]{1,0:T(8,128)(2,1)S(1)} collective-permute-done((bf16[128,1024]{1,0:T(8,128)(2,1)S(1)}, bf16[128,1024]{1,0:T(8,128)(2,1)S(1)}, u32[]{:S(2)}, u32[]{:S(2)}) %collective-permute-start.53) | collective-permute-done | bytes 262176 | tf_op jit(solution)/shard_map/ppermute | solution.py:53
  354.2 8.4 %attend_back.2 = (bf16[512,768]{1,0:T(8,128)(2,1)}, f32[2,256]{1,0:T(2,128)}, bf16[256,1024]{1,0:T(8,128)(2,1)}, f32[256,1024]{1,0:T(8,128)}) custom-call(bf16[128,1024]{1,0:T(8,128)(2,1)} %copy-done.23, bf16[128,1024]{1,0:T(8,128)(2,1)} %copy-done.46, bf16[128,1024]{1,0:T(8,128)(2,1)} %copy-done.47, bf16[128,1024]{1,0:T(8,128)(2,1)} %copy-done.48, ...), custom_call_target="tpu_custom_call" | custom-call | flops 2415919104 | bytes 8388608 | tf_op jit(solution)/shard_map/attend_back/pallas_call | solution.py:487
  367.8 7.3 %collective-permute-done.57.refs_3_ = bf16[128,1024]{1,0:T(8,128)(2,1)S(1)} collective-permute-done((bf16[128,1024]{1,0:T(8,128)(2,1)}, bf16[128,1024]{1,0:T(8,128)(2,1)S(1)}, u32[]{:S(2)}, u32[]{:S(2)}) %collective-permute-start.57) | collective-permute-done | bytes 262176 | tf_op jit(solution)/shard_map/ppermute | solution.py:53
  396.4 9.2 %ffn_back.3 = (bf16[512,1024]{1,0:T(8,128)(2,1)}, f32[1,1024]{1,0:T(1,128)}, bf16[256,1024]{1,0:T(8,128)(2,1)}, f32[256,1024]{1,0:T(8,128)}) custom-call(bf16[128,1024]{1,0:T(8,128)(2,1)} %copy-done.25, bf16[128,1024]{1,0:T(8,128)(2,1)} %copy-done.55, bf16[128,1024]{1,0:T(8,128)(2,1)} %copy-done.56, bf16[128,1024]{1,0:T(8,128)(2,1)} %copy-done.57, ...), custom_call_target="tpu_custom_call" | custom-call | flops 2147483648 | bytes 10485760 | tf_op jit(solution)/shard_map/ffn_back/pallas_call | solution.py:614
  422.1 9.0 %collective-permute-done.82 = bf16[24,128,128]{2,1,0:T(8,128)(2,1)} collective-permute-done((bf16[24,128,128]{2,1,0:T(8,128)(2,1)}, bf16[24,128,128]{2,1,0:T(8,128)(2,1)}, u32[]{:S(2)}, u32[]{:S(2)}) %collective-permute-start.82) | collective-permute-done | bytes 786464 | tf_op jit(solution)/shard_map/ppermute | solution.py:101
  438.4 8.4 %attend_back.3 = (bf16[512,768]{1,0:T(8,128)(2,1)}, f32[2,256]{1,0:T(2,128)}, bf16[256,1024]{1,0:T(8,128)(2,1)}, f32[256,1024]{1,0:T(8,128)}) custom-call(bf16[128,1024]{1,0:T(8,128)(2,1)} %copy-done.22, bf16[128,1024]{1,0:T(8,128)(2,1)} %copy-done.45, bf16[128,1024]{1,0:T(8,128)(2,1)} %copy-done.49, bf16[128,1024]{1,0:T(8,128)(2,1)} %copy-done.50, ...), custom_call_target="tpu_custom_call" | custom-call | flops 2415919104 | bytes 8388608 | tf_op jit(solution)/shard_map/attend_back/pallas_call | solution.py:487
  486.8 9.0 %collective-permute-done.72 = bf16[24,128,128]{2,1,0:T(8,128)(2,1)S(1)} collective-permute-done((bf16[24,128,128]{2,1,0:T(8,128)(2,1)}, bf16[24,128,128]{2,1,0:T(8,128)(2,1)S(1)}, u32[]{:S(2)}, u32[]{:S(2)}) %collective-permute-start.72) | collective-permute-done | bytes 786464 | tf_op jit(solution)/shard_map/ppermute | solution.py:101
  514.4 9.1 %collective-permute-done.86.refs_3_ = bf16[24,128,128]{2,1,0:T(8,128)(2,1)} collective-permute-done((bf16[24,128,128]{2,1,0:T(8,128)(2,1)}, bf16[24,128,128]{2,1,0:T(8,128)(2,1)}, u32[]{:S(2)}, u32[]{:S(2)}) %collective-permute-start.86) | collective-permute-done | bytes 786464 | tf_op jit(solution)/shard_map/ppermute | solution.py:237
  528.5 23.1 %collective-permute-done.94 = f32[2,12,1024]{2,1,0:T(8,128)S(1)} collective-permute-done((f32[2,12,1024]{2,1,0:T(8,128)S(1)}, f32[2,12,1024]{2,1,0:T(8,128)S(1)}, u32[]{:S(2)}, u32[]{:S(2)}) %collective-permute-start.94) | collective-permute-done | bytes 98336 | tf_op jit(solution)/shard_map/ppermute | solution.py:53
  560.3 8.2 %update.2 = (f32[2,24,128,128]{3,2,1,0:T(8,128)}, f32[2,24,128,128]{3,2,1,0:T(8,128)}, f32[2,24,128,128]{3,2,1,0:T(8,128)}, f32[2,24,128,128]{3,2,1,0:T(8,128)}) custom-call(bf16[24,128,128]{2,1,0:T(8,128)(2,1)S(1)} %copy-done.13, bf16[24,128,128]{2,1,0:T(8,128)(2,1)} %collective-permute-done.80.refs_1_, ...), custom_call_target="tpu_custom_call" | custom-call | flops 402653184 | bytes 17301504 | tf_op jit(solution)/shard_map/update/pallas_call | solution.py:718
  592.4 6.9 %collective-permute-done.75.refs_2_ = bf16[24,128,128]{2,1,0:T(8,128)(2,1)} collective-permute-done((bf16[24,128,128]{2,1,0:T(8,128)(2,1)}, bf16[24,128,128]{2,1,0:T(8,128)(2,1)}, u32[]{:S(2)}, u32[]{:S(2)}) %collective-permute-start.75) | collective-permute-done | bytes 786464 | tf_op jit(solution)/shard_map/ppermute | solution.py:110
  599.2 15.8 %collective-permute-done.76.refs_3_ = bf16[24,128,128]{2,1,0:T(8,128)(2,1)} collective-permute-done((bf16[24,128,128]{2,1,0:T(8,128)(2,1)}, bf16[24,128,128]{2,1,0:T(8,128)(2,1)}, u32[]{:S(2)}, u32[]{:S(2)}) %collective-permute-start.76) | collective-permute-done | bytes 786464 | tf_op jit(solution)/shard_map/ppermute | solution.py:237
  622.6 7.9 %update.3 = (f32[2,24,128,128]{3,2,1,0:T(8,128)}, f32[2,24,128,128]{3,2,1,0:T(8,128)}, f32[2,24,128,128]{3,2,1,0:T(8,128)}, f32[2,24,128,128]{3,2,1,0:T(8,128)}) custom-call(bf16[24,128,128]{2,1,0:T(8,128)(2,1)S(1)} %copy-done.14, ...), custom_call_target="tpu_custom_call", output_to_operand_aliasing={{0}: (11, {}), {1}: (12, {}), {2}: (13, {}), {3}: (14, {})} | custom-call | flops 402653184 | bytes 17301504 | tf_op jit(solution)/shard_map/update/pallas_call | solution.py:718
  (468 shorter events, 297.1 us)
Async XLA Ops:
  3.0 28.5 %collective-permute-start.5 = (bf16[24,128,128]{2,1,0:T(8,128)(2,1)S(1)}, bf16[24,128,128]{2,1,0:T(8,128)(2,1)S(1)}, u32[]{:S(2)}, u32[]{:S(2)}) collective-permute-start(bf16[24,128,128]{2,1,0:T(8,128)(2,1)S(1)} %get-tuple-element.110.refs_0_), channel_id=1, source_target_pairs={{0,8},{4,12},{8,16},{12,20},{16,24},{20,28},{1,9},{5,13},{9,17},{1... | collective-permute-start | bytes 2359304 | tf_op jit(solution)/shard_map/ppermute | solution.py:106
  9.4 42.1 %collective-permute-start.10 = (bf16[24,128,128]{2,1,0:T(8,128)(2,1)S(1)}, bf16[24,128,128]{2,1,0:T(8,128)(2,1)}, u32[]{:S(2)}, u32[]{:S(2)}) collective-permute-start(bf16[24,128,128]{2,1,0:T(8,128)(2,1)S(1)} %get-tuple-element.110.refs_0_), channel_id=1, source_target_pairs={{0,4},{4,0},{8,12},{12,8},{16,20},{20,16},{24,28},{28,24},{1,5},{5... | collective-permute-start | bytes 2359304 | tf_op jit(solution)/shard_map/ppermute | solution.py:101
  31.5 44.4 %collective-permute-start.9 = (bf16[24,128,128]{2,1,0:T(8,128)(2,1)S(1)}, bf16[24,128,128]{2,1,0:T(8,128)(2,1)}, u32[]{:S(2)}, u32[]{:S(2)}) collective-permute-start(bf16[24,128,128]{2,1,0:T(8,128)(2,1)S(1)} %get-tuple-element.110.refs_0_), channel_id=1, source_target_pairs={{0,24},{4,28},{24,0},{28,4},{1,25},{5,29},{25,1},{29,5},{2,26},{6,... | collective-permute-start | bytes 2359304 | tf_op jit(solution)/shard_map/ppermute | solution.py:110
  40.2 33.3 %collective-permute-start.8 = (bf16[24,128,128]{2,1,0:T(8,128)(2,1)}, bf16[24,128,128]{2,1,0:T(8,128)(2,1)}, u32[]{:S(2)}, u32[]{:S(2)}) collective-permute-start(bf16[24,128,128]{2,1,0:T(8,128)(2,1)} %collective-permute-done.6.refs_2_), channel_id=1, source_target_pairs={{16,8},{20,12},{8,0},{12,4},{17,9},{21,13},{9,1},{13,5},{18,10},{2... | collective-permute-start | bytes 2359304 | tf_op jit(solution)/shard_map/ppermute | solution.py:106
  50.8 29.3 %collective-permute-start.11 = (bf16[24,128,128]{2,1,0:T(8,128)(2,1)S(1)}, bf16[24,128,128]{2,1,0:T(8,128)(2,1)S(1)}, u32[]{:S(2)}, u32[]{:S(2)}) collective-permute-start(bf16[24,128,128]{2,1,0:T(8,128)(2,1)S(1)} %collective-permute-done.5.refs_1_), channel_id=1, source_target_pairs={{8,12},{12,8},{16,20},{20,16},{24,28},{28,24},{9,13},{13,9},{17,21... | collective-permute-start | bytes 2359304 | tf_op jit(solution)/shard_map/ppermute | solution.py:101
  51.5 29.4 %collective-permute-start.12 = (bf16[24,128,128]{2,1,0:T(8,128)(2,1)}, bf16[24,128,128]{2,1,0:T(8,128)(2,1)S(1)}, u32[]{:S(2)}, u32[]{:S(2)}) collective-permute-start(bf16[24,128,128]{2,1,0:T(8,128)(2,1)} %collective-permute-done.6.refs_2_), channel_id=1, source_target_pairs={{0,4},{4,0},{8,12},{12,8},{16,20},{20,16},{1,5},{5,1},{9,13},{13,9... | collective-permute-start | bytes 2359304 | tf_op jit(solution)/shard_map/ppermute | solution.py:101
  54.2 30.3 %collective-permute-start.13 = (bf16[24,128,128]{2,1,0:T(8,128)(2,1)}, bf16[24,128,128]{2,1,0:T(8,128)(2,1)}, u32[]{:S(2)}, u32[]{:S(2)}) collective-permute-start(bf16[24,128,128]{2,1,0:T(8,128)(2,1)} %collective-permute-done.7.refs_3_), channel_id=1, source_target_pairs={{16,20},{20,16},{24,28},{28,24},{17,21},{21,17},{25,29},{29,25},{1... | collective-permute-start | bytes 2359304 | tf_op jit(solution)/shard_map/ppermute | solution.py:101
  75.9 36.1 %collective-permute-start.15 = (bf16[24,128,128]{2,1,0:T(8,128)(2,1)}, bf16[24,128,128]{2,1,0:T(8,128)(2,1)}, u32[]{:S(2)}, u32[]{:S(2)}) collective-permute-start(bf16[24,128,128]{2,1,0:T(8,128)(2,1)} %collective-permute-done.9.refs_5_), channel_id=1, source_target_pairs={{0,4},{4,0},{24,28},{28,24},{1,5},{5,1},{25,29},{29,25},{2,6},{6,2... | collective-permute-start | bytes 2359304 | tf_op jit(solution)/shard_map/ppermute | solution.py:101
  80.9 41.5 %collective-permute-start.3 = (bf16[128,1024]{1,0:T(8,128)(2,1)S(1)}, bf16[128,1024]{1,0:T(8,128)(2,1)}, u32[]{:S(2)}, u32[]{:S(2)}) collective-permute-start(bf16[128,1024]{1,0:T(8,128)(2,1)S(1)} %convert_element_type.154.p0.refs_0_), channel_id=1, source_target_pairs={{0,1},{1,0},{2,3},{3,2},{4,5},{5,4},{6,7},{7,6},{8,9},{9,8},{10,11... | collective-permute-start | bytes 786440 | tf_op jit(solution)/shard_map/ppermute | solution.py:53
  81.8 40.6 %collective-permute-start.4 = (bf16[128,1024]{1,0:T(8,128)(2,1)S(1)}, bf16[128,1024]{1,0:T(8,128)(2,1)}, u32[]{:S(2)}, u32[]{:S(2)}) collective-permute-start(bf16[128,1024]{1,0:T(8,128)(2,1)S(1)} %collective-permute-done.2.p1.refs_1_), channel_id=1, source_target_pairs={{0,1},{1,0},{2,3},{3,2},{4,5},{5,4},{6,7},{7,6},{8,9},{9,8},{10,11... | collective-permute-start | bytes 786440 | tf_op jit(solution)/shard_map/ppermute | solution.py:53
  165.9 41.6 %collective-permute-start.29 = (bf16[24,128,128]{2,1,0:T(8,128)(2,1)S(1)}, bf16[24,128,128]{2,1,0:T(8,128)(2,1)S(1)}, u32[]{:S(2)}, u32[]{:S(2)}) collective-permute-start(bf16[24,128,128]{2,1,0:T(8,128)(2,1)S(1)} %collective-permute-done.27.refs_2_), channel_id=1, source_target_pairs={{16,8},{20,12},{8,0},{12,4},{17,9},{21,13},{9,1},{13,5},{18,10},{2... | collective-permute-start | bytes 2359304 | tf_op jit(solution)/shard_map/ppermute | solution.py:106
  167.2 41.0 %collective-permute-start.30 = (bf16[24,128,128]{2,1,0:T(8,128)(2,1)S(1)}, bf16[24,128,128]{2,1,0:T(8,128)(2,1)S(1)}, u32[]{:S(2)}, u32[]{:S(2)}) collective-permute-start(bf16[24,128,128]{2,1,0:T(8,128)(2,1)S(1)} %get-tuple-element.120.refs_0_), channel_id=1, source_target_pairs={{0,24},{4,28},{24,0},{28,4},{1,25},{5,29},{25,1},{29,5},{2,26},{6,... | collective-permute-start | bytes 2359304 | tf_op jit(solution)/shard_map/ppermute | solution.py:110
  174.0 40.9 %collective-permute-start.32 = (bf16[24,128,128]{2,1,0:T(8,128)(2,1)S(1)}, bf16[24,128,128]{2,1,0:T(8,128)(2,1)S(1)}, u32[]{:S(2)}, u32[]{:S(2)}) collective-permute-start(bf16[24,128,128]{2,1,0:T(8,128)(2,1)S(1)} %collective-permute-done.26.refs_1_), channel_id=1, source_target_pairs={{8,12},{12,8},{16,20},{20,16},{24,28},{28,24},{9,13},{13,9},{17,21... | collective-permute-start | bytes 2359304 | tf_op jit(solution)/shard_map/ppermute | solution.py:101
  175.8 35.1 %collective-permute-start.22 = (bf16[128,1024]{1,0:T(8,128)(2,1)S(1)}, bf16[128,1024]{1,0:T(8,128)(2,1)S(1)}, u32[]{:S(2)}, u32[]{:S(2)}) collective-permute-start(bf16[128,1024]{1,0:T(8,128)(2,1)S(1)} %add_convert_fusion.6), channel_id=1, source_target_pairs={{0,2},{1,3},{2,0},{3,1},{4,6},{5,7},{6,4},{7,5},{8,10},{9,11},{10,... | collective-permute-start | bytes 786440 | tf_op jit(solution)/shard_map/ppermute | solution.py:53
  176.4 39.0 %collective-permute-start.33 = (bf16[24,128,128]{2,1,0:T(8,128)(2,1)S(1)}, bf16[24,128,128]{2,1,0:T(8,128)(2,1)S(1)}, u32[]{:S(2)}, u32[]{:S(2)}) collective-permute-start(bf16[24,128,128]{2,1,0:T(8,128)(2,1)S(1)} %collective-permute-done.27.refs_2_), channel_id=1, source_target_pairs={{0,4},{4,0},{8,12},{12,8},{16,20},{20,16},{1,5},{5,1},{9,13},{13,9... | collective-permute-start | bytes 2359304 | tf_op jit(solution)/shard_map/ppermute | solution.py:101
  210.9 35.2 %collective-permute-start.36 = (bf16[24,128,128]{2,1,0:T(8,128)(2,1)S(1)}, bf16[24,128,128]{2,1,0:T(8,128)(2,1)S(1)}, u32[]{:S(2)}, u32[]{:S(2)}) collective-permute-start(bf16[24,128,128]{2,1,0:T(8,128)(2,1)S(1)} %collective-permute-done.30.refs_5_), channel_id=1, source_target_pairs={{0,4},{4,0},{24,28},{28,24},{1,5},{5,1},{25,29},{29,25},{2,6},{6,2... | collective-permute-start | bytes 2359304 | tf_op jit(solution)/shard_map/ppermute | solution.py:101
  215.4 45.3 %collective-permute-start.24 = (bf16[128,1024]{1,0:T(8,128)(2,1)S(1)}, bf16[128,1024]{1,0:T(8,128)(2,1)S(1)}, u32[]{:S(2)}, u32[]{:S(2)}) collective-permute-start(bf16[128,1024]{1,0:T(8,128)(2,1)S(1)} %get-tuple-element.118.p0.refs_0_), channel_id=1, source_target_pairs={{0,1},{1,0},{2,3},{3,2},{4,5},{5,4},{6,7},{7,6},{8,9},{9,8},{10,11... | collective-permute-start | bytes 786440 | tf_op jit(solution)/shard_map/ppermute | solution.py:53
  222.3 38.4 %collective-permute-start.25 = (bf16[128,1024]{1,0:T(8,128)(2,1)S(1)}, bf16[128,1024]{1,0:T(8,128)(2,1)S(1)}, u32[]{:S(2)}, u32[]{:S(2)}) collective-permute-start(bf16[128,1024]{1,0:T(8,128)(2,1)S(1)} %collective-permute-done.23.p1.refs_1_), channel_id=1, source_target_pairs={{0,1},{1,0},{2,3},{3,2},{4,5},{5,4},{6,7},{7,6},{8,9},{9,8},{10,11... | collective-permute-start | bytes 786440 | tf_op jit(solution)/shard_map/ppermute | solution.py:53
  416.1 61.6 %collective-permute-start.87 = (bf16[24,128,128]{2,1,0:T(8,128)(2,1)}, bf16[24,128,128]{2,1,0:T(8,128)(2,1)}, u32[]{:S(2)}, u32[]{:S(2)}) collective-permute-start(bf16[24,128,128]{2,1,0:T(8,128)(2,1)} %get-tuple-element.209), channel_id=1, source_target_pairs={{0,4},{4,0},{8,12},{12,8},{16,20},{20,16},{24,28},{28,24},{1,5},{5... | collective-permute-start | bytes 2359304 | tf_op jit(solution)/shard_map/ppermute | solution.py:101
  417.4 61.6 %collective-permute-start.81 = (bf16[24,128,128]{2,1,0:T(8,128)(2,1)}, bf16[24,128,128]{2,1,0:T(8,128)(2,1)}, u32[]{:S(2)}, u32[]{:S(2)}) collective-permute-start(bf16[24,128,128]{2,1,0:T(8,128)(2,1)} %get-tuple-element.211), channel_id=1, source_target_pairs={{0,4},{4,0},{8,12},{12,8},{16,20},{20,16},{24,28},{28,24},{1,5},{5... | collective-permute-start | bytes 2359304 | tf_op jit(solution)/shard_map/ppermute | solution.py:101
  433.6 45.4 %collective-permute-start.84 = (bf16[24,128,128]{2,1,0:T(8,128)(2,1)}, bf16[24,128,128]{2,1,0:T(8,128)(2,1)S(1)}, u32[]{:S(2)}, u32[]{:S(2)}) collective-permute-start(bf16[24,128,128]{2,1,0:T(8,128)(2,1)} %fusion.2), channel_id=1, source_target_pairs={{0,8},{4,12},{8,16},{12,20},{1,9},{5,13},{9,17},{13,21},{2,10},{6,... | collective-permute-start | bytes 2359304 | tf_op jit(solution)/shard_map/ppermute | solution.py:106
  477.8 34.6 %collective-permute-start.80 = (bf16[24,128,128]{2,1,0:T(8,128)(2,1)}, bf16[24,128,128]{2,1,0:T(8,128)(2,1)}, u32[]{:S(2)}, u32[]{:S(2)}) collective-permute-start(bf16[24,128,128]{2,1,0:T(8,128)(2,1)} %get-tuple-element.212), channel_id=1, source_target_pairs={{0,4},{4,0},{8,12},{12,8},{16,20},{20,16},{24,28},{28,24},{1,5},{5... | collective-permute-start | bytes 2359304 | tf_op jit(solution)/shard_map/ppermute | solution.py:101
  483.5 29.6 %collective-permute-start.85 = (bf16[24,128,128]{2,1,0:T(8,128)(2,1)}, bf16[24,128,128]{2,1,0:T(8,128)(2,1)}, u32[]{:S(2)}, u32[]{:S(2)}) collective-permute-start(bf16[24,128,128]{2,1,0:T(8,128)(2,1)} %get-tuple-element.206), channel_id=1, source_target_pairs={{0,24},{4,28},{24,0},{28,4},{1,25},{5,29},{25,1},{29,5},{2,26},{6,... | collective-permute-start | bytes 2359304 | tf_op jit(solution)/shard_map/ppermute | solution.py:110
  485.5 38.0 %collective-permute-start.86 = (bf16[24,128,128]{2,1,0:T(8,128)(2,1)}, bf16[24,128,128]{2,1,0:T(8,128)(2,1)}, u32[]{:S(2)}, u32[]{:S(2)}) collective-permute-start(bf16[24,128,128]{2,1,0:T(8,128)(2,1)} %get-tuple-element.206), channel_id=1, source_target_pairs={{8,0},{12,4},{16,24},{20,28},{9,1},{13,5},{17,25},{21,29},{10,2},{... | collective-permute-start | bytes 2359304 | tf_op jit(solution)/shard_map/ppermute | solution.py:237
  495.8 29.2 %collective-permute-start.88 = (bf16[24,128,128]{2,1,0:T(8,128)(2,1)}, bf16[24,128,128]{2,1,0:T(8,128)(2,1)}, u32[]{:S(2)}, u32[]{:S(2)}) collective-permute-start(bf16[24,128,128]{2,1,0:T(8,128)(2,1)} %get-tuple-element.205), channel_id=1, source_target_pairs={{0,8},{4,12},{8,16},{12,20},{1,9},{5,13},{9,17},{13,21},{2,10},{6,... | collective-permute-start | bytes 2359304 | tf_op jit(solution)/shard_map/ppermute | solution.py:106
  512.4 57.1 %collective-permute-start.77 = (bf16[24,128,128]{2,1,0:T(8,128)(2,1)}, bf16[24,128,128]{2,1,0:T(8,128)(2,1)S(1)}, u32[]{:S(2)}, u32[]{:S(2)}) collective-permute-start(bf16[24,128,128]{2,1,0:T(8,128)(2,1)} %get-tuple-element.214), channel_id=1, source_target_pairs={{0,4},{4,0},{8,12},{12,8},{16,20},{20,16},{24,28},{28,24},{1,5},{5... | collective-permute-start | bytes 2359304 | tf_op jit(solution)/shard_map/ppermute | solution.py:101
  513.1 57.9 %collective-permute-start.71 = (bf16[24,128,128]{2,1,0:T(8,128)(2,1)}, bf16[24,128,128]{2,1,0:T(8,128)(2,1)S(1)}, u32[]{:S(2)}, u32[]{:S(2)}) collective-permute-start(bf16[24,128,128]{2,1,0:T(8,128)(2,1)} %get-tuple-element.216), channel_id=1, source_target_pairs={{0,4},{4,0},{8,12},{12,8},{16,20},{20,16},{24,28},{28,24},{1,5},{5... | collective-permute-start | bytes 2359304 | tf_op jit(solution)/shard_map/ppermute | solution.py:101
  523.5 47.5 %collective-permute-start.74 = (bf16[24,128,128]{2,1,0:T(8,128)(2,1)}, bf16[24,128,128]{2,1,0:T(8,128)(2,1)S(1)}, u32[]{:S(2)}, u32[]{:S(2)}) collective-permute-start(bf16[24,128,128]{2,1,0:T(8,128)(2,1)} %fusion.7), channel_id=1, source_target_pairs={{0,8},{4,12},{8,16},{12,20},{1,9},{5,13},{9,17},{13,21},{2,10},{6,... | collective-permute-start | bytes 2359304 | tf_op jit(solution)/shard_map/ppermute | solution.py:106
  525.0 46.0 %collective-permute-start.73 = (bf16[24,128,128]{2,1,0:T(8,128)(2,1)}, bf16[24,128,128]{2,1,0:T(8,128)(2,1)S(1)}, u32[]{:S(2)}, u32[]{:S(2)}) collective-permute-start(bf16[24,128,128]{2,1,0:T(8,128)(2,1)} %fusion.7), channel_id=1, source_target_pairs={{24,16},{28,20},{16,8},{20,12},{25,17},{29,21},{17,9},{21,13},{26,... | collective-permute-start | bytes 2359304 | tf_op jit(solution)/shard_map/ppermute | solution.py:106
  576.7 38.3 %collective-permute-start.76 = (bf16[24,128,128]{2,1,0:T(8,128)(2,1)}, bf16[24,128,128]{2,1,0:T(8,128)(2,1)}, u32[]{:S(2)}, u32[]{:S(2)}) collective-permute-start(bf16[24,128,128]{2,1,0:T(8,128)(2,1)} %get-tuple-element.208), channel_id=1, source_target_pairs={{8,0},{12,4},{16,24},{20,28},{9,1},{13,5},{17,25},{21,29},{10,2},{... | collective-permute-start | bytes 2359304 | tf_op jit(solution)/shard_map/ppermute | solution.py:237
  578.0 37.0 %collective-permute-start.78 = (bf16[24,128,128]{2,1,0:T(8,128)(2,1)}, bf16[24,128,128]{2,1,0:T(8,128)(2,1)}, u32[]{:S(2)}, u32[]{:S(2)}) collective-permute-start(bf16[24,128,128]{2,1,0:T(8,128)(2,1)} %get-tuple-element.207), channel_id=1, source_target_pairs={{0,8},{4,12},{8,16},{12,20},{1,9},{5,13},{9,17},{13,21},{2,10},{6,... | collective-permute-start | bytes 2359304 | tf_op jit(solution)/shard_map/ppermute | solution.py:106
  584.3 30.7 %collective-permute-start.79 = (bf16[24,128,128]{2,1,0:T(8,128)(2,1)}, bf16[24,128,128]{2,1,0:T(8,128)(2,1)}, u32[]{:S(2)}, u32[]{:S(2)}) collective-permute-start(bf16[24,128,128]{2,1,0:T(8,128)(2,1)} %get-tuple-element.207), channel_id=1, source_target_pairs={{24,16},{28,20},{16,8},{20,12},{25,17},{29,21},{17,9},{21,13},{26,... | collective-permute-start | bytes 2359304 | tf_op jit(solution)/shard_map/ppermute | solution.py:106
  (152 other events, 1624.2 us)

commit v2 on v1

--- a/solution.py
+++ b/solution.py
@@ -23,8 +23,12 @@
     return [pl.BlockSpec(memory_space=pltpu.VMEM)] * count
 
 
-def params(mib=56):
+def params(mib=40):
     return pltpu.CompilerParams(vmem_limit_bytes=mib * 1024 * 1024)
+
+
+def cost(microseconds):
+    return pl.CostEstimate(flops=0, bytes_accessed=int(microseconds * 3.4e6), transcendentals=0)
 
 
 def shape(dims, dtype):
@@ -48,6 +52,12 @@
     )
 
 
+def flat_matrix(ref, base, rows, cols):
+    return jnp.concatenate(
+        [jnp.concatenate([ref[base + r * cols + c] for c in range(cols)], axis=1) for r in range(rows)], axis=0
+    )
+
+
 def swap(values, axis, flip):
     count = lax.axis_size(axis)
     return lax.ppermute(values, axis, [(i, i ^ flip) for i in range(count)])
@@ -63,37 +73,41 @@
 def scatter_sum(send, keep):
     rows = send.shape[0] // 2
     first = swap(send, "tensor", 1)
-    second = swap((keep[rows:] + first[rows:].astype(f32)).astype(bf16), "tensor", 2)
-    return (keep, first, second)
+    message = (keep[rows:] + first[rows:].astype(f32)).astype(bf16)
+    return (keep, first, swap(message, "tensor", 2)), message
+
+
+def by_index(relative):
+    index = lax.axis_index("tensor")
+    core, x_pos = index % 2 == 1, index // 2 == 1
+    r0, r1, r2, r3 = relative
+    a0, a1 = jnp.where(core, r1, r0), jnp.where(core, r0, r1)
+    a2, a3 = jnp.where(core, r3, r2), jnp.where(core, r2, r3)
+    return [
+        jnp.where(x_pos, a2, a0),
+        jnp.where(x_pos, a3, a1),
+        jnp.where(x_pos, a0, a2),
+        jnp.where(x_pos, a1, a3),
+    ]
 
 
 def to_tokens(values):
-    index = lax.axis_index("tensor")
-    x_pos, core = index // 2, index % 2
     rows, width = values.shape
-    half, quarter = rows // 2, rows // 4
-    mine = lax.dynamic_slice(values, (x_pos * half, 0), (half, width))
-    other = lax.dynamic_slice(values, ((1 - x_pos) * half, 0), (half, width))
-    pair = jnp.stack([mine, swap(other, "tensor", 2)])
-    keep = lax.dynamic_slice(pair, (0, core * quarter, 0), (2, quarter, width))
-    send = lax.dynamic_slice(pair, (0, (1 - core) * quarter, 0), (2, quarter, width))
-    got = swap(send, "tensor", 1)
-    relative = jnp.stack([keep[0], got[0], keep[1], got[1]])
-    ordered = jnp.take(relative, jnp.arange(4) ^ index, axis=0)
-    return ordered.transpose(1, 0, 2).reshape(quarter, 4 * width)
-
-
-def from_tokens(values):
-    index = lax.axis_index("tensor")
-    rows, wide = values.shape
-    width = wide // 4
-    groups = values.reshape(rows, 4, width).transpose(1, 0, 2)
-    relative = jnp.take(groups, jnp.arange(4) ^ index, axis=0)
-    got = swap(jnp.stack([relative[1], relative[3]]), "tensor", 1)
-    far = swap(jnp.stack([relative[2], got[1]]), "tensor", 2)
-    chunks = jnp.stack([relative[0], got[0], far[0], far[1]])
-    ordered = jnp.take(chunks, jnp.arange(4) ^ index, axis=0)
-    return ordered.reshape(4 * rows, width)
+    quarter = rows // 4
+    r0, r1, r2, r3 = by_index([values[g * quarter : (g + 1) * quarter] for g in range(4)])
+    got = swap(jnp.stack([r2, r3]), "tensor", 2)
+    near = swap(jnp.stack([r1, got[1]]), "tensor", 1)
+    return jnp.concatenate(by_index([r0, near[0], got[0], near[1]]), axis=1)
+
+
+def from_tokens(values, marks=None):
+    width = values.shape[1] // 4
+    r0, r1, r2, r3 = by_index([values[:, g * width : (g + 1) * width] for g in range(4)])
+    near = jnp.stack([r1, r3])
+    got = swap(near if marks is None else after(near, marks[0]), "tensor", 1)
+    rest = jnp.stack([r2, got[1]])
+    far = swap(rest if marks is None else after(rest, marks[1]), "tensor", 2)
+    return jnp.concatenate(by_index([r0, got[0], far[0], far[1]]), axis=0)
 
 
 def cross(values, planes):
@@ -114,89 +128,94 @@
     return lax.optimization_barrier((values,) + tuple(others))[0]
 
 
-def spread_blocks(own):
-    up_one = hop(own, (0, 1, 2), 1)
-    down_one = hop(own, (1, 2, 3), -1)
-    own_y = cross(own, (0, 1, 2, 3))
-    up_two = hop(up_one, (1, 2), 1)
-    down_two = hop(down_one, (2, 1), -1)
-    ends = ends_swap(after(own, up_one, down_one))
-    up_one_y = cross(up_one, (1, 2, 3))
-    down_one_y = cross(down_one, (0, 1, 2))
-    up_two_y = cross(up_two, (2, 3))
-    down_two_y = cross(down_two, (0, 1))
-    ends_y = cross(ends, (0, 3))
+def line_steps(plane):
+    middle = (plane == 1) | (plane == 2)
+    two = jnp.where(plane >= 2, -2, 2)
     return (
-        (own, up_one, down_one, up_two, down_two, ends),
-        (own_y, up_one_y, down_one_y, up_two_y, down_two_y, ends_y),
-    )
-
-
-def source_table(inverse, slots):
-    dp_index = lax.axis_index("dp")
-    plane, column = dp_index // 2, dp_index % 2
-    end_step = 3 - 2 * plane
-    steps = jnp.stack([0 * plane, plane * 0 - 1, plane * 0 + 1, plane * 0 - 2, plane * 0 + 2, end_step])
-    target = plane + steps
-    valid = (target >= 0) & (target <= 3)
-    valid = valid.at[5].set((plane == 0) | (plane == 3))
-    both_target = jnp.concatenate([target * 2 + column, target * 2 + 1 - column])
-    both_valid = jnp.concatenate([valid, valid])
-    picked = jnp.take(inverse.reshape(8, slots), jnp.clip(both_target, 0, 7), axis=0)
-    return jnp.where(both_valid[:, None], picked, -1).astype(jnp.int32)
-
-
-def assemble_kernel(source_count, slots, table, *refs):
-    sources, out, sem = refs[:source_count], refs[source_count], refs[source_count + 1]
-    for j in range(source_count):
-
-        @pl.when(table[j, 0] >= 0)
-        def _(j=j):
-            @pl.loop(0, slots)
-            def _(s):
-                pltpu.make_async_copy(sources[j].at[s], out.at[table[j, s]], sem).start()
-
-    for j in range(source_count):
-
-        @pl.when(table[j, 0] >= 0)
-        def _(j=j):
-            @pl.loop(0, slots)
-            def _(s):
-                pltpu.make_async_copy(sources[j].at[s], out.at[table[j, s]], sem).wait()
-
-
-def assemble(sources, table, total):
-    slots, side = sources[0].shape[0], sources[0].shape[1]
-    count = len(sources)
-    return pl.pallas_call(
-        functools.partial(assemble_kernel, count, slots),
-        grid_spec=pltpu.PrefetchScalarGridSpec(
-            num_scalar_prefetch=1,
-            grid=(),
-            in_specs=[pl.BlockSpec(memory_space=pl.ANY)] * count,
-            out_specs=pl.BlockSpec(memory_space=pl.ANY),
-            scratch_shapes=[pltpu.SemaphoreType.DMA],
-        ),
-        out_shape=shape((total, side, side), bf16),
-        compiler_params=params(8),
-        cost_estimate=pl.CostEstimate(flops=0, bytes_accessed=4 * total * side * side, transcendentals=0),
-        name="assemble",
-    )(table, *sources)
-
-
-def gather_weights(own, owner_row):
-    total = owner_row.shape[0]
-    slots = own.shape[0]
+        0 * plane,
+        jnp.where(plane == 0, 1, -1),
+        jnp.where(middle, 1, two),
+        jnp.where(middle, two, 3 - 2 * plane),
+    )
+
+
+def middle_plane(plane):
+    return (plane == 1) | (plane == 2)
+
+
+def weight_sources(own, owner_map, meanwhile):
+    layers, total = owner_map.shape
+    slots = own[0].shape[0]
     positions = jnp.arange(total, dtype=jnp.int32)
-    hits = owner_row[None, :] == positions[:, None]
-    inverse = jnp.sum(jnp.where(hits, positions[None, :], 0), axis=1)
-    if lax.axis_size("dp") == 8:
-        straight, crossed = spread_blocks(own)
-        table = source_table(inverse, slots)
-        last = crossed[-1]
-        return assemble(straight + crossed, table, total), last
-    whole = lax.all_gather(own, "dp", axis=0, tiled=True)
-    return assemble((whole,), inverse[None, :].astype(jnp.int32), total), whole
+    hits = owner_map[:, None, :] == positions[None, :, None]
+    inverse = jnp.sum(jnp.where(hits, positions[None, None, :], 0), axis=2).astype(jnp.int32)
+    if lax.axis_size("dp") != 8:
+        wholes = [lax.all_gather(values.astype(bf16), "dp", axis=0, tiled=True) for values in own]
+        for stage in range(3):
+            meanwhile(stage, None)
+        return [((whole,), ((0, 0),), row[None, :]) for whole, row in zip(wholes, inverse)], None
+    plane, column = lax.axis_index("dp") // 2, lax.axis_index("dp") % 2
+    middle = middle_plane(plane)
+    everywhere = (0, 1, 2, 3)
+    spots = tuple((j, 0) for j in range(8))
+    tables = []
+    for layer in range(layers):
+        owners = inverse[layer].reshape(8, slots)
+        rows = []
+        for side in (column, 1 - column):
+            for step in line_steps(plane):
+                mask = jnp.arange(8) == (plane + step) * 2 + side
+                rows.append(jnp.sum(jnp.where(mask[:, None], owners, 0), axis=0))
+        tables.append(jnp.stack(rows).astype(jnp.int32))
+
+    first = own[0].astype(bf16)
+    up_one = hop(first, (0, 1, 2), 1)
+    down_one = hop(first, (1, 2, 3), -1)
+    first_y = cross(first, everywhere)
+    beside = meanwhile(0, None)
+    done = (up_one, down_one, first_y) + beside[0]
+    one = jnp.where(plane == 0, down_one, up_one)
+    up_two = hop(after(up_one, *done), (1, 2), 1)
+    down_two = hop(after(down_one, *done), (2, 1), -1)
+    one_y = cross(after(one, *done), everywhere)
+    beside += meanwhile(1, first_y)
+    done = (up_two, down_two, one_y) + beside[1]
+    two = up_two + down_two
+    third = jnp.where(middle, down_one, after(two, one_y))
+    ends = ends_swap(after(first, *done))
+    third_y = cross(after(third, *done), everywhere)
+    beside += meanwhile(2, one_y)
+    done = (ends, third_y) + beside[2]
+    last = jnp.where(middle, after(two, third_y), ends)
+    last_y = cross(after(last, *done), everywhere)
+    result = [((first, one, third, last, first_y, one_y, third_y, last_y), spots, tables[0])]
+    points = {}
+
+    for layer in range(1, layers):
+        mine = after(own[layer], first_y).astype(bf16)
+        start = after(mine, *done)
+        up_one = hop(start, (0, 1, 2), 1)
+        down_one = hop(start, (1, 2, 3), -1)
+        one = jnp.where(plane == 0, down_one, up_one)
+        up_two = hop(up_one, (1, 2), 1)
+        down_two = hop(down_one, (2, 1), -1)
+        mine_y = cross(after(mine, last_y), everywhere)
+        two = up_two + down_two
+        third = jnp.where(middle, after(down_one, one), two)
+        ends = ends_swap(after(mine, up_two, down_two))
+        one_y = cross(after(one, mine_y), everywhere)
+        last = jnp.where(middle, after(two, third), ends)
+        third_y = cross(after(third, one_y), everywhere)
+        half = slots // 2
+        inner_y = lax.ppermute(after(mine_y, ends), "dp", [(0, 4), (1, 5), (6, 2), (7, 3)])
+        ends_y = ends_swap(after(mine_y, ends)[:half])
+        rest_y = cross(after(ends, third_y)[half:], (0, 3))
+        last_y = inner_y + jnp.concatenate([ends_y, rest_y])
+        result.append(((mine, one, third, last, mine_y, one_y, third_y, last_y), spots, tables[layer]))
+        if layer == 1:
+            points.update(start=(up_one, down_one), attend=(up_two, down_two, mine_y), hidden=(ends, one_y))
+        done = (last_y, third_y)
+    return result, points
 
 
 def send_positions(owner_row, slots):
@@ -204,41 +223,52 @@
         return owner_row
     dp_index = lax.axis_index("dp")
     plane, column = dp_index // 2, dp_index % 2
-    order = jnp.array([[3, 2, 1, 0], [0, 3, 2, 1], [1, 2, 3, 0], [0, 1, 2, 3]], jnp.int32)
+    order = ((3, 2, 0, 1), (1, 3, 2, 0), (0, 2, 3, 1), (1, 0, 2, 3))
     owner = owner_row // slots
-    place = jnp.take(jnp.take(order, plane, axis=0), owner // 2)
+    place = jnp.zeros_like(owner)
+    for sender in range(4):
+        for receiver in range(4):
+            hit = (plane == sender) & (owner // 2 == receiver)
+            place = jnp.where(hit, order[sender][receiver], place)
     side = (owner % 2 == column).astype(jnp.int32)
-    return ((place * 2 + side) * slots + owner_row % slots).astype(jnp.int32)
-
-
-def reduce_blocks(grads, slots):
-    if lax.axis_size("dp") != 8:
-        return (lax.psum_scatter(grads, "dp", scatter_dimension=0, tiled=True),)
-    side = grads.shape[-1]
-    parts = grads.reshape(4, 2, slots, side, side)
+    return ((side * 4 + place) * slots + owner_row % slots).astype(jnp.int32)
+
+
+def reduce_blocks(parts, small=None):
+    if len(parts) == 1:
+        if small is not None:
+            small = lax.psum(small, "dp")
+        return (lax.psum_scatter(parts[0], "dp", scatter_dimension=0, tiled=True),), small, None
     plane = lax.axis_index("dp") // 2
     everywhere = (0, 1, 2, 3)
-    got = {}
-    for k in (1, 0, 2, 3):
-        got[k] = cross(parts[k, 0], everywhere)
-
-    def total(k, *more):
-        value = parts[k, 1].astype(f32) + got[k].astype(f32)
+    sending, staying = parts[:-4], parts[-4:]
+    low = plane == 1
+
+    def total(k, got, *more, then=()):
+        value = after(staying[k], *then).astype(f32) + got.astype(f32)
         for extra in more:
             value = value + extra.astype(f32)
         return value.astype(bf16)
 
-    two = total(1)
-    up_two = hop(two, (0, 1), 1)
-    down_two = hop(two, (3, 2), -1)
-    low = plane == 1
-    near = total(0, jnp.where(low, down_two, up_two))
+    def two_away(value):
+        return hop(value, (0, 1), 1), hop(value, (3, 2), -1)
+
+    def to_near(value):
+        return lax.ppermute(value, "dp", [(2, 0), (3, 1), (4, 6), (5, 7)])
+
+    got = [cross(sending[0], everywhere)]
+    small = small + swap(small, "dp", 2)
+    small = small + swap(small, "dp", 4)
+    got.append(cross(after(sending[1], got[0], small), everywhere))
+    up, down = two_away(total(0, got[0]))
+    small = small + swap(after(small, got[0]), "dp", 1)
+    got.append(cross(after(sending[2], got[1], up, down, small), everywhere))
+    near = total(1, got[1], jnp.where(low, down, up))
     ends = ends_swap(near)
-    out_near = lax.ppermute(near, "dp", [(2, 0), (3, 1), (4, 6), (5, 7)])
-    far = total(2, jnp.where(low, up_two, down_two))
-    up_one = hop(far, (0, 1), 1)
-    down_one = hop(far, (3, 2), -1)
-    return (parts[3, 1], got[3], ends, out_near, up_one, down_one)
+    got.append(cross(after(sending[3], got[2], ends), everywhere))
+    far = total(2, got[2], jnp.where(low, up, down), then=(near,))
+    mine = (staying[3], got[3], ends, to_near(after(near, ends)), *two_away(far))
+    return mine, small, got
 
 
 def norm_kernel(base, keep, first, second, vec, low_out, full_out, normed_out, scale_out, *, rows):
@@ -286,8 +316,8 @@
         in_specs=[whole_spec(base), top_half(keep), top_half(first), whole_spec(second), whole_spec(vec)],
         out_specs=[whole_spec(o) for o in outs],
         out_shape=outs,
-        compiler_params=params(24),
-        cost_estimate=pl.CostEstimate(flops=20 * tokens * width, bytes_accessed=20 * tokens * width, transcendentals=tokens),
+        compiler_params=params(12),
+        cost_estimate=cost(1.2),
         name="norm",
     )(base, keep, first, second, vec)
 
@@ -328,8 +358,8 @@
         in_specs=specs,
         out_specs=[whole_spec(o) for o in outs],
         out_shape=outs,
-        compiler_params=params(24),
-        cost_estimate=pl.CostEstimate(flops=20 * tokens * width, bytes_accessed=20 * tokens * width, transcendentals=0),
+        compiler_params=params(12),
+        cost_estimate=cost(1.5),
         name="norm_back",
     )(*operands)
 
@@ -340,22 +370,47 @@
     keep_out[...] = total[:half]
 
 
+def start_blocks(sources, spots, table, stage, sem):
+    slots = table.shape[1]
+    for row, (which, first) in enumerate(spots):
+
+        @pl.loop(0, slots, unroll=min(slots, 24))
+        def _(s, row=row, which=which, first=first):
+            pltpu.make_async_copy(sources[which].at[first + s], stage.at[table[row, s]], sem).start()
+
+
 def attend_kernel(
-    p0, p1, p2, p3, w_qkv, w_out, vec, seg_col, seg_row,
-    query_out, key_out, value_out, mix_out, log_out, send_out, keep_out, bias,
+    count, spots, n_qkv, n_out, table, *refs
 ):
+    sources = refs[:count]
+    (
+        p0, p1, p2, p3, vec, seg_col, seg_row,
+        query_out, key_out, value_out, mix_out, log_out, send_out, keep_out, attend_out, ffn_out,
+        bias, stage, sems,
+    ) = refs[count:]
+    start_blocks(sources, spots, table, stage, sems.at[0])
     wide = cat_rows((p0, p1, p2, p3))
+    bias[...] = jnp.where(seg_col[...] == seg_row[...], 0.0, -1e30)
+    pltpu.make_async_copy(stage, stage, sems.at[0]).wait()
+    cut = n_qkv + n_out
+    copies = (
+        pltpu.make_async_copy(stage.at[pl.ds(0, cut)], attend_out, sems.at[1]),
+        pltpu.make_async_copy(stage.at[pl.ds(cut, ffn_out.shape[0])], ffn_out, sems.at[2]),
+    )
+    for copy in copies:
+        copy.start()
     tokens, model = wide.shape
     width = query_out.shape[1]
-    tile = w_qkv.shape[-1]
-    projected = jnp.dot(wide, matrix(w_qkv, model // tile, 3 * width // tile), preferred_element_type=f32)
+    tile = stage.shape[-1]
+    projected = jnp.dot(
+        wide, flat_matrix(stage, 0, model // tile, 3 * width // tile), preferred_element_type=f32
+    )
     query = (projected[:, :width] + vec[0:1, :]).astype(bf16) * jnp.asarray(HD**-0.5, bf16)
     keys = projected[:, width : 2 * width].astype(bf16)
     values = (projected[:, 2 * width :] + vec[1:2, :]).astype(bf16)
     query_out[...] = query
     key_out[...] = keys
     value_out[...] = values
-    bias[...] = jnp.where(seg_col[...] == seg_row[...], 0.0, -1e30)
     lane = lax.broadcasted_iota(jnp.int32, (tokens, 128), 1)
     logs = jnp.zeros((tokens, 128), f32)
     mixes = []
@@ -379,19 +434,25 @@
     mixture = jnp.concatenate(mixes, axis=1)
     mix_out[...] = mixture
     log_out[...] = jnp.transpose(logs)[0:8, :]
-    total = jnp.dot(mixture, matrix(w_out, width // tile, model // tile), preferred_element_type=f32)
+    total = jnp.dot(
+        mixture, flat_matrix(stage, n_qkv, width // tile, model // tile), preferred_element_type=f32
+    )
     store_sums(total, send_out, keep_out)
+    for copy in copies:
+        copy.wait()
 
 
 def block_rows(array, start, count):
     return pl.BlockSpec((count,) + tuple(array.shape[1:]), lambda i: (start // count, 0, 0, 0))
 
 
-def attend_step(pieces, blocks, counts, vec, seg_col, seg_row):
+def attend_step(pieces, weights, counts, vec, seg_col, seg_row):
     quarter, model = pieces[0].shape
     tokens, width = 4 * quarter, vec.shape[1]
     n_qkv, n_out, n_up = counts
-    per = blocks.shape[1]
+    arrays, spots, table = weights
+    side = arrays[0].shape[-1]
+    total = n_qkv + n_out + 2 * n_up
     outs = [
         shape((tokens, width), bf16),
         shape((tokens, width), bf16),
@@ -400,24 +461,28 @@
         shape((8, tokens), f32),
         shape((tokens // 2, model), bf16),
         shape((tokens // 2, model), f32),
+        shape((n_qkv + n_out, side, side), bf16),
+        shape((2 * n_up, side, side), bf16),
     ]
+    operands = list(pieces) + [vec, seg_col, seg_row]
     return pl.pallas_call(
-        attend_kernel,
-        grid=(1,),
-        in_specs=[whole_spec(p) for p in pieces]
-        + [block_rows(blocks, 0, n_qkv // per), block_rows(blocks, n_qkv // per, n_out // per)]
-        + [whole_spec(vec), whole_spec(seg_col), whole_spec(seg_row)],
-        out_specs=[whole_spec(o) for o in outs],
+        functools.partial(attend_kernel, len(arrays), spots, n_qkv, n_out),
+        grid_spec=pltpu.PrefetchScalarGridSpec(
+            num_scalar_prefetch=1,
+            grid=(),
+            in_specs=[pl.BlockSpec(memory_space=pl.ANY)] * len(arrays) + vmem_spec(len(operands)),
+            out_specs=vmem_spec(7) + [pl.BlockSpec(memory_space=pl.ANY)] * 2,
+            scratch_shapes=[
+                pltpu.VMEM((tokens, tokens), f32),
+                pltpu.VMEM((total, side, side), bf16),
+                pltpu.SemaphoreType.DMA((3,)),
+            ],
+        ),
         out_shape=outs,
-        scratch_shapes=[pltpu.VMEM((tokens, tokens), f32)],
-        compiler_params=params(),
-        cost_estimate=pl.CostEstimate(
-            flops=2 * tokens * model * 4 * width + 4 * tokens * tokens * width * 2,
-            bytes_accessed=8 * 1024 * 1024,
-            transcendentals=tokens * tokens * width // HD,
-        ),
+        compiler_params=params(60),
+        cost_estimate=cost(11),
         name="attend",
-    )(*pieces, blocks, blocks, vec, seg_col, seg_row)
+    )(table, *arrays, *operands)
 
 
 def attend_back_kernel(
@@ -494,11 +559,7 @@
         out_shape=outs,
         scratch_shapes=[pltpu.VMEM((tokens, tokens), f32)],
         compiler_params=params(),
-        cost_estimate=pl.CostEstimate(
-            flops=2 * tokens * model * 4 * width + 10 * tokens * tokens * width * 2,
-            bytes_accessed=8 * 1024 * 1024,
-            transcendentals=tokens * tokens * width // HD,
-        ),
+        cost_estimate=cost(6.5),
         name="attend_back",
     )(*pieces, blocks, blocks, query, keys, values, logs, seg_col, seg_row)
 
@@ -538,9 +599,9 @@
     n_qkv, n_out, n_up = counts
     per = blocks.shape[1]
     side = blocks.shape[2]
-    up_row = (n_qkv + n_out) // per
+    up_row = 0
     up_rows = n_up // per
-    down_row = (n_qkv + n_out + n_up) // per
+    down_row = n_up // per
     up_spec = pl.BlockSpec((up_rows, chunk_blocks, side, side), lambda i: (up_row // up_rows, i, 0, 0))
     down_spec = pl.BlockSpec((chunk_blocks, per, side, side), lambda i: (down_row // chunk_blocks + i, 0, 0, 0))
     return up_spec, down_spec
@@ -567,9 +628,7 @@
         out_shape=outs,
         scratch_shapes=[pltpu.VMEM((tokens, model), f32)],
         compiler_params=params(),
-        cost_estimate=pl.CostEstimate(
-            flops=4 * tokens * model * hidden, bytes_accessed=10 * 1024 * 1024, transcendentals=2 * tokens * hidden
-        ),
+        cost_estimate=cost(7.5),
         name="ffn",
     )(*pieces, blocks, blocks, up_bias)
 
@@ -619,22 +678,13 @@
         out_shape=outs,
         scratch_shapes=[pltpu.VMEM((tokens, model), f32)],
         compiler_params=params(),
-        cost_estimate=pl.CostEstimate(
-            flops=4 * tokens * model * hidden, bytes_accessed=10 * 1024 * 1024, transcendentals=0
-        ),
+        cost_estimate=cost(7),
         name="ffn_back",
     )(*pieces, blocks, blocks, slope)
 
 
-def weight_grad_kernel(jobs, chained, place, *refs):
-    counts = [count for job in jobs for count in job[:2]]
-    used = sum(counts)
-    operands, rest = refs[:used], refs[used + chained :]
-    out, stage, sem = rest
-    side = stage.shape[-1]
+def weight_grad_jobs(jobs, operands, side, store):
     at = 0
-    done = []
-    slot = 0
     for left_count, right_count, base in jobs:
         left = operands[at : at + left_count]
         right = operands[at + left_count : at + left_count + right_count]
@@ -648,44 +698,87 @@
             result = lax.dot_general(rows, columns, FIRST, preferred_element_type=f32).astype(bf16)
             for i in range(chunk // side):
                 for j in range(per):
-                    block = base + (start // side + i) * per + j
-                    stage[slot] = result[i * side : (i + 1) * side, j * side : (j + 1) * side]
-                    pltpu.make_async_copy(stage.at[slot], out.at[place[block]], sem).start()
-                    done.append((slot, block))
-                    slot += 1
-    for slot, block in done:
-        pltpu.make_async_copy(stage.at[slot], out.at[place[block]], sem).wait()
-
-
-def weight_grad_step(jobs, place, target, total, side):
+                    store(
+                        base + (start // side + i) * per + j,
+                        result[i * side : (i + 1) * side, j * side : (j + 1) * side],
+                    )
+
+
+def job_parts(jobs, side):
     operands = [a for left, right, base in jobs for a in left + right]
     layout = tuple((len(left), len(right), base) for left, right, base in jobs)
-    blocks = sum(
-        left[0].shape[1] // side * (right[0].shape[1] // side) for left, right, base in jobs
-    )
-    chained = 0 if target is None else 1
-    extra = [] if target is None else [target]
-    aliases = {} if target is None else {1 + len(operands): 0}
+    blocks = sum(left[0].shape[1] // side * (right[0].shape[1] // side) for left, right, base in jobs)
     tokens = sum(a.shape[0] for a in jobs[0][0])
+    return operands, layout, blocks, tokens
+
+
+def first_grad_kernel(jobs, used, place, *refs):
+    out = refs[used]
+
+    def store(block, value):
+        out[place[block]] = value
+
+    weight_grad_jobs(jobs, refs[:used], out.shape[-1], store)
+
+
+def first_grad_step(jobs, place, total, side):
+    operands, layout, blocks, tokens = job_parts(jobs, side)
     return pl.pallas_call(
-        functools.partial(weight_grad_kernel, layout, chained),
+        functools.partial(first_grad_kernel, layout, len(operands)),
         grid_spec=pltpu.PrefetchScalarGridSpec(
             num_scalar_prefetch=1,
             grid=(),
-            in_specs=vmem_spec(len(operands)) + [pl.BlockSpec(memory_space=pl.ANY)] * chained,
-            out_specs=pl.BlockSpec(memory_space=pl.ANY),
-            scratch_shapes=[pltpu.VMEM((blocks, side, side), bf16), pltpu.SemaphoreType.DMA],
+            in_specs=vmem_spec(len(operands)),
+            out_specs=pl.BlockSpec(memory_space=pltpu.VMEM),
         ),
         out_shape=shape((total, side, side), bf16),
-        input_output_aliases=aliases,
-        compiler_params=params(),
-        cost_estimate=pl.CostEstimate(
-            flops=2 * tokens * blocks * side * side,
-            bytes_accessed=4 * blocks * side * side,
-            transcendentals=0,
+        compiler_params=params(60),
+        cost_estimate=cost(4),
+        name="first_grad",
+    )(place, *operands)
+
+
+def last_grad_kernel(jobs, used, sizes, place, *refs):
+    operands, earlier = refs[:used], refs[used]
+    outs, stage, sems = refs[used + 1 : used + 1 + len(sizes)], refs[-2], refs[-1]
+    side = stage.shape[-1]
+    load = pltpu.make_async_copy(earlier, stage, sems.at[0])
+    load.start()
+    waited = []
+
+    def store(block, value):
+        if not waited:
+            load.wait()
+            waited.append(block)
+        stage[place[block]] = value
+
+    weight_grad_jobs(jobs, operands, side, store)
+    copies, first = [], 0
+    for k, size in enumerate(sizes):
+        copies.append(pltpu.make_async_copy(stage.at[pl.ds(first, size)], outs[k], sems.at[1 + k]))
+        copies[-1].start()
+        first += size
+    for copy in copies:
+        copy.wait()
+
+
+def last_grad_step(jobs, earlier, place, total, side, sizes):
+    count = len(sizes)
+    operands, layout, blocks, tokens = job_parts(jobs, side)
+    return pl.pallas_call(
+        functools.partial(last_grad_kernel, layout, len(operands), tuple(sizes)),
+        grid_spec=pltpu.PrefetchScalarGridSpec(
+            num_scalar_prefetch=1,
+            grid=(),
+            in_specs=vmem_spec(len(operands)) + [pl.BlockSpec(memory_space=pl.ANY)],
+            out_specs=[pl.BlockSpec(memory_space=pl.ANY)] * count,
+            scratch_shapes=[pltpu.VMEM((total, side, side), bf16), pltpu.SemaphoreType.DMA((1 + count,))],
         ),
-        name="weight_grad",
-    )(place, *operands, *extra)
+        out_shape=[shape((size, side, side), bf16) for size in sizes],
+        compiler_params=params(60),
+        cost_estimate=cost(8),
+        name="last_grad",
+    )(place, *operands, earlier)
 
 
 def update_kernel(part_count, chained, *refs):
@@ -724,22 +817,15 @@
         out_specs=[one] * 4,
         out_shape=[shape(state[0].shape, f32)] * 4,
         input_output_aliases=aliases,
-        compiler_params=params(32),
-        cost_estimate=pl.CostEstimate(
-            flops=8 * slots * side**3, bytes_accessed=44 * slots * side * side, transcendentals=0
-        ),
+        compiler_params=params(60),
+        cost_estimate=cost(10),
         name="update",
     )(*parts, *state, *chained)
 
 
-def sum_all(values):
-    if lax.axis_size("dp") != 8:
-        return lax.psum(values, ("dp", "tensor"))
+def sum_tensor(values):
     values = values + swap(values, "tensor", 1)
-    values = values + swap(values, "tensor", 2)
-    values = values + swap(values, "dp", 1)
-    values = values + swap(values, "dp", 2)
-    return values + swap(values, "dp", 4)
+    return values + swap(values, "tensor", 2)
 
 
 def body(
@@ -768,79 +854,135 @@
     index = lax.axis_index("tensor")
     quarter = tokens // 4
 
-    low = [masters[layer].astype(bf16) for layer in range(layers)]
+    segments = jnp.concatenate(
+        by_index([segment_ids[:, g * quarter : (g + 1) * quarter] for g in range(4)]), axis=1
+    )
+    segments = jnp.concatenate(
+        [segments[:, g * quarter : (g + 1) * quarter] for g in (0, 2, 1, 3)], axis=1
+    )
+    seg_col, seg_row = segments.reshape(tokens, 1), segments
+    places = [send_positions(owner_map[layer], slots) for layer in range(layers)]
+
+    made = {}
+
+    def meanwhile(stage, mark):
+        def hold(values):
+            return values if mark is None else after(values, mark)
+
+        if stage == 0:
+            near = swap(vectors, "tensor", 1)
+            far = swap(jnp.stack([vectors, near]), "tensor", 2)
+            made["vectors"] = jnp.concatenate(by_index([vectors, near, far[0], far[1]]), axis=2)
+            made["stream"] = to_tokens(layer_in)
+            made["places"] = tuple(
+                send_positions(owner_map[layer], slots) if layer == 0 else owner_map[layer] for layer in range(layers)
+            )
+            part = (made["vectors"], made["stream"]) + made["places"]
+        elif stage == 1:
+            made["wide"] = gather_tokens(hold(made["stream"]).astype(bf16))
+            part = made["wide"] + (seg_col,)
+        else:
+            made["grad"] = to_tokens(hold(cotangent))
+            part = (made["grad"],)
+        return (part,)
+
+    own = [masters[layer] for layer in range(layers)]
+    sources, points = weight_sources(own, owner_map, meanwhile)
+    paired = points is not None
+    wide_vectors, stream, wide_in, grad, places = (
+        made[name] for name in ("vectors", "stream", "wide", "grad", "places")
+    )
     weights = []
-    last = None
-    for layer in range(layers):
-        own = low[layer] if last is None else after(low[layer], last)
-        gathered, last = gather_weights(own, owner_map[layer])
-        weights.append(gathered.reshape(total // tile_rows, tile_rows, side, side))
-
-    order = jnp.array([0, 2, 1, 3]) ^ index
-    segments = jnp.take(segment_ids.reshape(4, quarter), order, axis=0).reshape(tokens)
-    seg_col, seg_row = segments[:, None], segments[None, :]
-    wide_vectors = lax.all_gather(vectors, "tensor", axis=2, tiled=True)
-
-    stream = to_tokens(layer_in)
-    stream_low = stream.astype(bf16)
-    grad = to_tokens(cotangent)
+    if paired:
+        sources[0] = sources[0][:2] + (after(sources[0][2], *points["start"]),)
 
     kept = []
     for layer in range(layers):
-        vec, blocks = wide_vectors[layer], weights[layer]
-        wide_in = gather_tokens(stream_low)
-        query, keys, values, mixture, logs, send, keep = attend_step(
-            wide_in, blocks, counts, vectors[layer], seg_col, seg_row
+        vec = wide_vectors[layer]
+        if layer > 0:
+            wide_in = gather_tokens(stream_low)
+        query, keys, values, mixture, logs, send, keep, attend_blocks, ffn_blocks = attend_step(
+            wide_in, sources[layer], counts, vectors[layer], seg_col, seg_row
         )
-        mid_low, middle, normed_one, scale_one = norm_step(stream, scatter_sum(send, keep), vec, (2, 3, 4))
+        attend_blocks = attend_blocks.reshape(-1, tile_rows, side, side)
+        ffn_blocks = ffn_blocks.reshape(-1, tile_rows, side, side)
+        weights.append((attend_blocks, ffn_blocks))
+        if layer == 0 and paired:
+            send = after(send, *points["attend"])
+        sums, message = scatter_sum(send, keep)
+        mid_low, middle, normed_one, scale_one = norm_step(stream, sums, vec, (2, 3, 4))
         wide_mid = gather_tokens(mid_low)
-        activated, slope, send, keep = ffn_step(wide_mid, blocks, counts, up_bias[layer : layer + 1])
-        stream_low, stream, normed_two, scale_two = norm_step(middle, scatter_sum(send, keep), vec, (5, 6, 7))
+        activated, slope, send, keep = ffn_step(wide_mid, ffn_blocks, counts, up_bias[layer : layer + 1])
+        if layer == 0 and paired:
+            send = after(send, *points["hidden"])
+        stream_low, stream, normed_two, scale_two = norm_step(middle, scatter_sum(send, keep)[0], vec, (5, 6, 7))
         kept.append(
             (wide_in, query, keys, values, mixture, logs, normed_one, scale_one, wide_mid, activated, slope, normed_two, scale_two)
         )
-    layer_out = from_tokens(stream)
 
     vector_sums = [None] * layers
     bias_sums = [None] * layers
     state = (masters, left_stats, right_stats, left_roots, right_roots)
     updated = None
     sums = None
+    waiting = []
     for layer in reversed(range(layers)):
-        vec, blocks = wide_vectors[layer], weights[layer]
+        vec, (attend_blocks, ffn_blocks) = wide_vectors[layer], weights[layer]
         (wide_in, query, keys, values, mixture, logs, normed_one, scale_one, wide_mid, activated, slope, normed_two, scale_two) = kept[layer]
-        place = send_positions(owner_map[layer], slots)
+        first = layer == 0 and paired
         grad_low, grad_two, sums_two = norm_back_step(grad, sums, normed_two, scale_two, vec, 6)
         wide_grad = gather_tokens(grad_low)
-        grad_pre, bias_sum, send, keep = ffn_back_step(wide_grad, blocks, counts, slope)
-        sums = scatter_sum(send, keep)
-        block_grads = weight_grad_step(
-            [((wide_mid), (grad_pre,), n_qkv + n_out), ((activated,), (wide_grad), n_qkv + n_out + n_up)],
-            place, None, total, side,
+        grad_pre, bias_sum, send, keep = ffn_back_step(wide_grad, ffn_blocks, counts, slope)
+        sums, message = scatter_sum(send, keep)
+        ffn_grads = None if first else first_grad_step(
+            [(wide_mid, (grad_pre,), n_qkv + n_out), ((activated,), wide_grad, n_qkv + n_out + n_up)],
+            after(places[layer], message), total, side,
         )
+        if not first:
+            sums = (after(sums[0], ffn_grads),) + sums[1:]
         grad_low, grad_one, sums_one = norm_back_step(grad_two, sums, normed_one, scale_one, vec, 3)
         wide_first = gather_tokens(grad_low)
+        if first:
+            ffn_grads = first_grad_step(
+                [(wide_mid, (grad_pre,), n_qkv + n_out), ((activated,), wide_grad, n_qkv + n_out + n_up)],
+                after(places[layer], grad_low), total, side,
+            )
+            wide_first = wide_first[:1] + (after(wide_first[1], ffn_grads),) + wide_first[2:]
         grad_qkv, qv_sums, send, keep = attend_back_step(
-            wide_first, blocks, counts, query, keys, values, logs, seg_col, seg_row
+            wide_first, attend_blocks, counts, query, keys, values, logs, seg_col, seg_row
         )
-        sums = scatter_sum(send, keep)
-        block_grads = weight_grad_step(
-            [((wide_in), (grad_qkv,), 0), ((mixture,), (wide_first), n_qkv)],
-            place, block_grads, total, side,
+        sums, message = scatter_sum(send, keep)
+        sizes = [total]
+        if paired:
+            sizes = [total // 8] * 8 if layer == 0 else [total]
+        block_parts = last_grad_step(
+            [(wide_in, (grad_qkv,), 0), ((mixture,), wide_first, n_qkv)],
+            ffn_grads, places[layer] if first else after(places[layer], message), total, side, sizes,
         )
         grad = grad_one
-        parts = reduce_blocks(block_grads, slots)
-        updated = update_step(parts, layer, state, updated)
+        if layer > 0:
+            sums = (after(sums[0], *block_parts),) + sums[1:]
         spread = jnp.concatenate([jnp.zeros_like(sums_one[:2]), sums_one, sums_two], axis=0)
         vector_sums[layer] = lax.dynamic_update_slice(spread, qv_sums, (0, index * width))
         bias_sums[layer] = lax.dynamic_update_slice(
             jnp.zeros((1, 4 * hidden), f32), bias_sum, (0, index * hidden)
         ).reshape(4 * hidden // model, model)
+        small = None
+        if layer == 0:
+            small = jnp.stack([jnp.concatenate(pair, axis=0) for pair in zip(vector_sums, bias_sums)])
+            small = sum_tensor(small)
+        parts, small, crossed = reduce_blocks(block_parts, small)
+        waiting.append((parts, layer))
     input_grad = from_tokens(
-        grad + sums[0][:quarter] + sums[1][:quarter].astype(f32) + sums[2].astype(f32)
-    )
-
-    small = sum_all(jnp.stack([jnp.concatenate(pair, axis=0) for pair in zip(vector_sums, bias_sums)]))
+        grad + sums[0][:quarter] + sums[1][:quarter].astype(f32) + sums[2].astype(f32), crossed
+    )
+    layer_out = from_tokens(stream, crossed)
+    for parts, layer in waiting:
+        if layer > 0 and paired:
+            state = (after(masters, crossed[1]),) + state[1:]
+        updated = update_step(parts, layer, state, updated)
+        state = (masters,) + state[1:]
+
     vector_grads = lax.dynamic_slice(small[:, :8], (0, 0, index * width), (layers, 8, width))
     up_bias_grads = lax.dynamic_slice(
         small[:, 8:].reshape(layers, 4 * hidden), (0, index * hidden), (layers, hidden)

time: 642 us -> 514 us (0.80)
  waiting for transfers between devices: 280 us -> 238 us
  local copies, waits for them, and re-layouts: 65.1 us -> 32.8 us
  starting transfers between devices: 106 us -> 79.4 us
  other arithmetic: 45.8 us -> 24.8 us
  between operations: 2.59 us -> 16.2 us
  Pallas kernels: 125 us -> 114 us
  blocking collectives: 6.7 us -> 0 us
    ppermute x53 -> x55, waiting for transfers between devices: 127 us -> 157 us  [swap(): return lax.ppermute(values, axis, [(i, i ^ flip) for i in range(count)])]
    ppermute x20 -> x12, waiting for transfers between devices: 72.7 us -> 48.6 us  [cross(): return lax.ppermute(values, 'dp', pairs)]
    ppermute x2, waiting for transfers between devices: 24.9 us -> 1.77 us  [the longest x1 1.77 us: to_near(): return lax.ppermute(value, 'dp', [(2, 0), (3, 1), (4, 6), (5, 7)])]
    ppermute x16 -> x12, waiting for transfers between devices: 48.4 us -> 26.7 us  [hop(): return lax.ppermute(values, 'dp', pairs)]
    ppermute x20 -> x12, starting transfers between devices: 30.5 us -> 15.4 us  [cross(): return lax.ppermute(values, 'dp', pairs)]
    unnamed x180 -> x218, local copies, waits for them, and re-layouts: 37.4 us -> 23 us
    convert_element_type x4 -> x3, other arithmetic: 12.5 us -> 1.27 us  [total(): return value.astype(bf16)]
    gather x10 -> x0, local copies, waits for them, and re-layouts: 10.3 us -> none  [the longest x2 3.8 us: from_tokens(): ordered = jnp.take(chunks, jnp.arange(4) ^ index, axis=0)]
  transfers between devices with their start and end apart: 95 -> 86, of which waited for: 41 -> 50; matrix products, arithmetic and copies ran while one was open for 10% -> 6% of each run, Pallas kernels for 10% -> 13%
where the time goes in v2:
time: 514 us; the launch traced here: 504 us
  waiting for transfers between devices  238 us (46%)
  Pallas kernels  114 us (22%)
  starting transfers between devices  79.4 us (15%)
  local copies, waits for them, and re-layouts  32.8 us (6%)
  other arithmetic  24.8 us (5%)
  between operations  16.2 us (3%)
    ppermute x55, waiting for transfers between devices, swap(): return lax.ppermute(values, axis, [(i, i ^ flip) for i in range(count)])  157 us
    ppermute x12, waiting for transfers between devices, cross(): return lax.ppermute(values, 'dp', pairs)  48.6 us
    ppermute x12, waiting for transfers between devices, hop(): return lax.ppermute(values, 'dp', pairs)  26.7 us
    ppermute x55, starting transfers between devices, swap(): return lax.ppermute(values, axis, [(i, i ^ flip) for i in range(count)])  25.2 us
    ppermute x12, starting transfers between devices, hop(): return lax.ppermute(values, 'dp', pairs)  23.8 us
    unnamed x218, local copies, waits for them, and re-layouts  23 us
    pallas_call x2, Pallas kernels, attend_step(): pl.pallas_call(functools.partial(attend_kernel, len(arrays), spots, n_qkv...  19.5 us
    pallas_call x2, Pallas kernels, update_step(): pl.pallas_call(functools.partial(update_kernel, len(parts), len(chained))...  18.9 us
  transfers between devices with their start and end apart: 86, of which 50 were waited for; matrix products, arithmetic and copies ran while one was open for 6% of the time, Pallas kernels for 13%

profile of v2, /device:TPU:0, one launch (start us, length us, event | category | flops | bytes accessed | tf_op | source)
XLA Modules:
  0.0 504.4 jit_solution(12724498929681168532)
XLA Ops:
  48.3 12.8 %collective-permute-done.8 = bf16[24,128,128]{2,1,0:T(8,128)(2,1)} collective-permute-done((bf16[24,128,128]{2,1,0:T(8,128)(2,1)S(1)}, bf16[24,128,128]{2,1,0:T(8,128)(2,1)}, u32[]{:S(2)}, u32[]{:S(2)}) %collective-permute-start.8) | collective-permute-done | bytes 786464 | tf_op jit(solution)/shard_map/ppermute | solution.py:120
  72.4 10.2 %collective-permute-done.14.refs_6_ = bf16[24,128,128]{2,1,0:T(8,128)(2,1)S(1)} collective-permute-done((bf16[24,128,128]{2,1,0:T(8,128)(2,1)S(1)}, bf16[24,128,128]{2,1,0:T(8,128)(2,1)S(1)}, u32[]{:S(2)}, u32[]{:S(2)}) %collective-permute-start.14) | collective-permute-done | bytes 786464 | tf_op jit(solution)/shard_map/ppermute | solution.py:115
  93.0 11.3 %collective-permute-done.19.refs_7_ = bf16[24,128,128]{2,1,0:T(8,128)(2,1)} collective-permute-done((bf16[24,128,128]{2,1,0:T(8,128)(2,1)S(1)}, bf16[24,128,128]{2,1,0:T(8,128)(2,1)}, u32[]{:S(2)}, u32[]{:S(2)}) %collective-permute-start.19) | collective-permute-done | bytes 786464 | tf_op jit(solution)/shard_map/ppermute | solution.py:115
  111.4 9.8 %attend.2 = (bf16[512,256]{1,0:T(8,128)(2,1)}, bf16[512,256]{1,0:T(8,128)(2,1)}, bf16[512,256]{1,0:T(8,128)(2,1)}, bf16[512,256]{1,0:T(8,128)(2,1)}, f32[8,512]{...) custom-call(s32[8,24]{1,0:T(8,128)} %stack.145.table, ...), custom_call_target="tpu_custom_call" | custom-call | bytes 37400000 | tf_op jit(solution)/shard_map/attend/pallas_call | solution.py:468
  139.9 7.0 %collective-permute-done.25.p1.refs_1_ = bf16[128,1024]{1,0:T(8,128)(2,1)S(1)} collective-permute-done((bf16[128,1024]{1,0:T(8,128)(2,1)S(1)}, bf16[128,1024]{1,0:T(8,128)(2,1)S(1)}, u32[]{:S(2)}, u32[]{:S(2)}) %collective-permute-start.25) | collective-permute-done | bytes 262176 | tf_op jit(solution)/shard_map/ppermute | solution.py:63
  148.4 6.7 %ffn.2 = (bf16[512,1024]{1,0:T(8,128)(2,1)S(1)}, f32[512,1024]{1,0:T(8,128)S(1)}, bf16[256,1024]{1,0:T(8,128)(2,1)S(1)}, f32[256,1024]{1,0:T(8,128)S(1)}) custom-call(bf16[128,1024]{1,0:T(8,128)(2,1)S(1)} %get-tuple-element.153.p0.refs_0_, bf16[128,1024]{1,0:T(8,128)(2,1)S(1)} %collective-permute-done.25.p1.refs_1_, ...), custom_call_target="tpu_custom_call" | custom-call | bytes 25500000 | tf_op jit(solution)/shard_map/ffn/pallas_call | solution.py:622
  169.2 9.7 %collective-permute-done.32.refs_6_ = bf16[24,128,128]{2,1,0:T(8,128)(2,1)S(1)} collective-permute-done((bf16[24,128,128]{2,1,0:T(8,128)(2,1)S(1)}, bf16[24,128,128]{2,1,0:T(8,128)(2,1)S(1)}, u32[]{:S(2)}, u32[]{:S(2)}) %collective-permute-start.32) | collective-permute-done | bytes 786464 | tf_op jit(solution)/shard_map/ppermute | solution.py:115
  195.4 9.7 %attend.3 = (bf16[512,256]{1,0:T(8,128)(2,1)}, bf16[512,256]{1,0:T(8,128)(2,1)}, bf16[512,256]{1,0:T(8,128)(2,1)}, bf16[512,256]{1,0:T(8,128)(2,1)}, f32[8,512]{...) custom-call(s32[8,24]{1,0:T(8,128)} %stack.162.table, ...), custom_call_target="tpu_custom_call" | custom-call | bytes 37400000 | tf_op jit(solution)/shard_map/attend/pallas_call | solution.py:468
  209.0 7.8 %collective-permute-done.40.second = bf16[128,1024]{1,0:T(8,128)(2,1)S(1)} collective-permute-done((bf16[128,1024]{1,0:T(8,128)(2,1)S(1)}, bf16[128,1024]{1,0:T(8,128)(2,1)S(1)}, u32[]{:S(2)}, u32[]{:S(2)}) %collective-permute-start.40) | collective-permute-done | bytes 262176 | tf_op jit(solution)/shard_map/ppermute | solution.py:63
  219.0 7.0 %collective-permute-done.41.p1.refs_1_ = bf16[128,1024]{1,0:T(8,128)(2,1)S(1)} collective-permute-done((bf16[128,1024]{1,0:T(8,128)(2,1)S(1)}, bf16[128,1024]{1,0:T(8,128)(2,1)S(1)}, u32[]{:S(2)}, u32[]{:S(2)}) %collective-permute-start.41) | collective-permute-done | bytes 262176 | tf_op jit(solution)/shard_map/ppermute | solution.py:63
  229.8 6.7 %ffn.3 = (bf16[512,1024]{1,0:T(8,128)(2,1)S(1)}, f32[512,1024]{1,0:T(8,128)S(1)}, bf16[256,1024]{1,0:T(8,128)(2,1)S(1)}, f32[256,1024]{1,0:T(8,128)S(1)}) custom-call(bf16[128,1024]{1,0:T(8,128)(2,1)S(1)} %get-tuple-element.170.p0.refs_0_, bf16[128,1024]{1,0:T(8,128)(2,1)S(1)} %collective-permute-done.41.p1.refs_1_, ...), custom_call_target="tpu_custom_call" | custom-call | bytes 25500000 | tf_op jit(solution)/shard_map/ffn/pallas_call | solution.py:622
  239.2 7.8 %collective-permute-done.45.second = bf16[128,1024]{1,0:T(8,128)(2,1)S(1)} collective-permute-done((bf16[128,1024]{1,0:T(8,128)(2,1)S(1)}, bf16[128,1024]{1,0:T(8,128)(2,1)S(1)}, u32[]{:S(2)}, u32[]{:S(2)}) %collective-permute-start.45) | collective-permute-done | bytes 262176 | tf_op jit(solution)/shard_map/ppermute | solution.py:63
  248.9 7.0 %collective-permute-done.46.p1.refs_7_ = bf16[128,1024]{1,0:T(8,128)(2,1)S(1)} collective-permute-done((bf16[128,1024]{1,0:T(8,128)(2,1)S(1)}, bf16[128,1024]{1,0:T(8,128)(2,1)S(1)}, u32[]{:S(2)}, u32[]{:S(2)}) %collective-permute-start.46) | collective-permute-done | bytes 262176 | tf_op jit(solution)/shard_map/ppermute | solution.py:63
  257.5 6.7 %ffn_back.2 = (bf16[512,1024]{1,0:T(8,128)(2,1)S(1)}, f32[1,1024]{1,0:T(1,128)S(1)}, bf16[256,1024]{1,0:T(8,128)(2,1)S(1)}, f32[256,1024]{1,0:T(8,128)S(1)}) custom-call(bf16[128,1024]{1,0:T(8,128)(2,1)S(1)} %get-tuple-element.178.p0.refs_6_, bf16[128,1024]{1,0:T(8,128)(2,1)S(1)} %collective-permute-done.46.p1.refs_7_, ...), custom_call_target="tpu_custom_call" | custom-call | bytes 23800000 | tf_op jit(solution)/shard_map/ffn_back/pallas_call | solution.py:673
  268.5 8.0 %first_grad.2.refs_10_ = bf16[192,128,128]{2,1,0:T(8,128)(2,1)} custom-call(s32[192]{0:T(256)} %bitcast.171, bf16[128,1024]{1,0:T(8,128)(2,1)} %copy-done.25, bf16[128,1024]{1,0:T(8,128)(2,1)} %copy-done.26, bf16[128,1024]{1,0:T(8,128)(2,1)} %copy-done.27, bf16[128,1024]{1,0:T(8,128)(2,1)} %copy-done.29, bf16[512,1024]{1,0:T(8,128)(2,1)} %copy-done.40, ...), custom_call_target="tpu_custom_call" | custom-call | bytes 13600000 | tf_op jit(solution)/shard_map/first_grad/pallas_call | solution.py:726
  281.1 6.6 %collective-permute-done.51.p1.refs_7_ = bf16[128,1024]{1,0:T(8,128)(2,1)S(1)} collective-permute-done((bf16[128,1024]{1,0:T(8,128)(2,1)S(1)}, bf16[128,1024]{1,0:T(8,128)(2,1)S(1)}, u32[]{:S(2)}, u32[]{:S(2)}) %collective-permute-start.51) | collective-permute-done | bytes 262176 | tf_op jit(solution)/shard_map/ppermute | solution.py:63
  290.3 5.2 %attend_back.2 = (bf16[512,768]{1,0:T(8,128)(2,1)S(1)}, f32[2,256]{1,0:T(2,128)S(1)}, bf16[256,1024]{1,0:T(8,128)(2,1)S(1)}, f32[256,1024]{1,0:T(8,128)S(1)}) custom-call(bf16[128,1024]{1,0:T(8,128)(2,1)S(1)} %get-tuple-element.189.p0.refs_6_, bf16[128,1024]{1,0:T(8,128)(2,1)S(1)} %collective-permute-done.51.p1.refs_7_, ...), custom_call_target="tpu_custom_call" | custom-call | bytes 22100000 | tf_op jit(solution)/shard_map/attend_back/pallas_call | solution.py:552
  297.6 9.2 %last_grad.2 = bf16[192,128,128]{2,1,0:T(8,128)(2,1)} custom-call(s32[192]{0:T(256)} %bitcast.172, bf16[128,1024]{1,0:T(8,128)(2,1)} %copy-done.10, bf16[128,1024]{1,0:T(8,128)(2,1)} %copy-done.83, bf16[128,1024]{1,0:T(8,128)(2,1)} %copy-done.84, bf16[128,1024]{1,0:T(8,128)(2,1)} %copy-done.85, bf16[512,768]{1,0:T(8,128)(2,1)} %copy-done.41, ...), custom_call_target="tpu_custom_call" | custom-call | bytes 27200000 | tf_op jit(solution)/shard_map/last_grad/pallas_call | solution.py:768
  308.4 6.8 %collective-permute-done.55.refs_3_ = bf16[128,1024]{1,0:T(8,128)(2,1)S(1)} collective-permute-done((bf16[128,1024]{1,0:T(8,128)(2,1)S(1)}, bf16[128,1024]{1,0:T(8,128)(2,1)S(1)}, u32[]{:S(2)}, u32[]{:S(2)}) %collective-permute-start.55) | collective-permute-done | bytes 262176 | tf_op jit(solution)/shard_map/ppermute | solution.py:63
  318.3 6.0 %collective-permute-done.56.p1.refs_7_ = bf16[128,1024]{1,0:T(8,128)(2,1)S(1)} collective-permute-done((bf16[128,1024]{1,0:T(8,128)(2,1)S(1)}, bf16[128,1024]{1,0:T(8,128)(2,1)S(1)}, u32[]{:S(2)}, u32[]{:S(2)}) %collective-permute-start.56) | collective-permute-done | bytes 262176 | tf_op jit(solution)/shard_map/ppermute | solution.py:63
  328.2 6.5 %ffn_back.3 = (bf16[512,1024]{1,0:T(8,128)(2,1)S(1)}, f32[1,1024]{1,0:T(1,128)S(1)}, bf16[256,1024]{1,0:T(8,128)(2,1)S(1)}, f32[256,1024]{1,0:T(8,128)S(1)}) custom-call(bf16[128,1024]{1,0:T(8,128)(2,1)S(1)} %get-tuple-element.204.p0.refs_6_, bf16[128,1024]{1,0:T(8,128)(2,1)S(1)} %collective-permute-done.56.p1.refs_7_, ...), custom_call_target="tpu_custom_call" | custom-call | bytes 23800000 | tf_op jit(solution)/shard_map/ffn_back/pallas_call | solution.py:673
  338.4 6.9 %collective-permute-done.60.refs_3_ = bf16[128,1024]{1,0:T(8,128)(2,1)S(1)} collective-permute-done((bf16[128,1024]{1,0:T(8,128)(2,1)S(1)}, bf16[128,1024]{1,0:T(8,128)(2,1)S(1)}, u32[]{:S(2)}, u32[]{:S(2)}) %collective-permute-start.60) | collective-permute-done | bytes 262176 | tf_op jit(solution)/shard_map/ppermute | solution.py:63
  353.5 8.1 %first_grad.3.refs_10_ = bf16[192,128,128]{2,1,0:T(8,128)(2,1)} custom-call(s32[192]{0:T(256)} %fusion.10.place, bf16[128,1024]{1,0:T(8,128)(2,1)} %copy-done.15, bf16[128,1024]{1,0:T(8,128)(2,1)} %copy-done.16, bf16[128,1024]{1,0:T(8,128)(2,1)} %copy-done.17, bf16[128,1024]{1,0:T(8,128)(2,1)} %copy-done.18, bf16[512,1024]{1,0:T(8,128)(2,1)} %copy-done.38, ...), custom_call_target="tpu_custom_call" | custom-call | bytes 13600000 | tf_op jit(solution)/shard_map/first_grad/pallas_call | solution.py:726
  364.6 5.2 %attend_back.3 = (bf16[512,768]{1,0:T(8,128)(2,1)S(1)}, f32[2,256]{1,0:T(2,128)S(1)}, bf16[256,1024]{1,0:T(8,128)(2,1)S(1)}, f32[256,1024]{1,0:T(8,128)S(1)}) custom-call(bf16[128,1024]{1,0:T(8,128)(2,1)S(1)} %get-tuple-element.210.p0.refs_6_, bf16[128,1024]{1,0:T(8,128)(2,1)S(1)} %collective-permute-done.61.p1.refs_7_, ...), custom_call_target="tpu_custom_call" | custom-call | bytes 22100000 | tf_op jit(solution)/shard_map/attend_back/pallas_call | solution.py:552
  374.9 9.6 %last_grad.3 = (bf16[24,128,128]{2,1,0:T(8,128)(2,1)}, bf16[24,128,128]{2,1,0:T(8,128)(2,1)}, bf16[24,128,128]{2,1,0:T(8,128)(2,1)}, bf16[24,128,128]{2,1,0:T(8,...) custom-call(s32[192]{0:T(256)} %fusion.10.place, ...), custom_call_target="tpu_custom_call" | custom-call | bytes 27200000 | tf_op jit(solution)/shard_map/last_grad/pallas_call | solution.py:768
  386.1 5.8 %collective-permute-done.68 = f32[2,12,1024]{2,1,0:T(8,128)S(1)} collective-permute-done((f32[2,12,1024]{2,1,0:T(8,128)S(1)}, f32[2,12,1024]{2,1,0:T(8,128)S(1)}, u32[]{:S(2)}, u32[]{:S(2)}) %collective-permute-start.68) | collective-permute-done | bytes 98336 | tf_op jit(solution)/shard_map/ppermute | solution.py:63
  392.0 16.9 %collective-permute-done.69 = f32[2,12,1024]{2,1,0:T(8,128)S(1)} collective-permute-done((f32[2,12,1024]{2,1,0:T(8,128)S(1)}, f32[2,12,1024]{2,1,0:T(8,128)S(1)}, u32[]{:S(2)}, u32[]{:S(2)}) %collective-permute-start.69) | collective-permute-done | bytes 98336 | tf_op jit(solution)/shard_map/ppermute | solution.py:63
  418.1 19.9 %collective-permute-done.78 = f32[2,12,1024]{2,1,0:T(8,128)S(1)} collective-permute-done((f32[2,12,1024]{2,1,0:T(8,128)S(1)}, f32[2,12,1024]{2,1,0:T(8,128)S(1)}, u32[]{:S(2)}, u32[]{:S(2)}) %collective-permute-start.78) | collective-permute-done | bytes 98336 | tf_op jit(solution)/shard_map/ppermute | solution.py:63
  447.5 11.5 %collective-permute-done.79 = bf16[24,128,128]{2,1,0:T(8,128)(2,1)S(1)} collective-permute-done((bf16[24,128,128]{2,1,0:T(8,128)(2,1)S(1)}, bf16[24,128,128]{2,1,0:T(8,128)(2,1)S(1)}, u32[]{:S(2)}, u32[]{:S(2)}) %collective-permute-start.79) | collective-permute-done | bytes 786464 | tf_op jit(solution)/shard_map/ppermute | solution.py:115
  459.5 5.2 %collective-permute-start.83 = (bf16[24,128,128]{2,1,0:T(8,128)(2,1)S(1)}, bf16[24,128,128]{2,1,0:T(8,128)(2,1)S(1)}, u32[]{:S(2)}, u32[]{:S(2)}) collective-permute-start(bf16[24,128,128]{2,1,0:T(8,128)(2,1)S(1)} %add_convert_fusion), channel_id=1, source_target_pairs={{0,8},{4,12},{8,16},{12,20},{1,9},{5,13},{9,17},{13,21},{2,10},{6,... | collective-permute-start | bytes 2359304 | tf_op jit(solution)/shard_map/ppermute | solution.py:120
  475.7 8.8 %update.2 = (f32[2,24,128,128]{3,2,1,0:T(8,128)}, f32[2,24,128,128]{3,2,1,0:T(8,128)}, f32[2,24,128,128]{3,2,1,0:T(8,128)}, f32[2,24,128,128]{3,2,1,0:T(8,128)}) custom-call(bf16[24,128,128]{2,1,0:T(8,128)(2,1)} %reduce-scatter.2.cloned.1.call-done.refs_0_, f32[2,24,128,128]{3,2,1,0:T(8,128)} %refs_6_.1, f32[2,24,128,128]{3,2,1,0:T(8,128)} %refs_7_.1, ...), custom_call_target="tpu_custom_call" | custom-call | bytes 34000000 | tf_op jit(solution)/shard_map/update/pallas_call | solution.py:811
  487.1 10.2 %update.3 = (f32[2,24,128,128]{3,2,1,0:T(8,128)}, f32[2,24,128,128]{3,2,1,0:T(8,128)}, f32[2,24,128,128]{3,2,1,0:T(8,128)}, f32[2,24,128,128]{3,2,1,0:T(8,128)}) custom-call(bf16[24,128,128]{2,1,0:T(8,128)(2,1)} %get-tuple-element.240.refs_0_, ...), custom_call_target="tpu_custom_call", output_to_operand_aliasing={{0}: (11, {}), {1}: (12, {}), {2}: (13, {}), {3}: (14, {})} | custom-call | bytes 34000000 | tf_op jit(solution)/shard_map/update/pallas_call | solution.py:811
  (478 shorter events, 211.9 us)
Async XLA Ops:
  7.2 468.5 %reduce-scatter.2.cloned.1.call-start = ((), (), s32[]{:S(2)}) async-start(), calls=%async_computation.1 | async-start | bytes 7077888 | tf_op jit(solution)/shard_map/reduce_scatter | solution.py:241
  10.4 20.5 %collective-permute-start.2 = (bf16[24,128,128]{2,1,0:T(8,128)(2,1)S(1)}, bf16[24,128,128]{2,1,0:T(8,128)(2,1)S(1)}, u32[]{:S(2)}, u32[]{:S(2)}) collective-permute-start(bf16[24,128,128]{2,1,0:T(8,128)(2,1)S(1)} %get-tuple-element.140.refs_0_), channel_id=1, source_target_pairs={{0,4},{4,0},{8,12},{12,8},{16,20},{20,16},{24,28},{28,24},{1,5},{5... | collective-permute-start | bytes 2359304 | tf_op jit(solution)/shard_map/ppermute | solution.py:115
  13.3 20.0 %collective-permute-start.3 = (bf16[24,128,128]{2,1,0:T(8,128)(2,1)S(1)}, bf16[24,128,128]{2,1,0:T(8,128)(2,1)}, u32[]{:S(2)}, u32[]{:S(2)}) collective-permute-start(bf16[24,128,128]{2,1,0:T(8,128)(2,1)S(1)} %get-tuple-element.140.refs_0_), channel_id=1, source_target_pairs={{0,8},{4,12},{8,16},{12,20},{16,24},{20,28},{1,9},{5,13},{9,17},{1... | collective-permute-start | bytes 2359304 | tf_op jit(solution)/shard_map/ppermute | solution.py:120
  17.7 20.6 %collective-permute-start.4 = (bf16[24,128,128]{2,1,0:T(8,128)(2,1)S(1)}, bf16[24,128,128]{2,1,0:T(8,128)(2,1)S(1)}, u32[]{:S(2)}, u32[]{:S(2)}) collective-permute-start(bf16[24,128,128]{2,1,0:T(8,128)(2,1)S(1)} %get-tuple-element.140.refs_0_), channel_id=1, source_target_pairs={{8,0},{12,4},{16,8},{20,12},{24,16},{28,20},{9,1},{13,5},{17,9},{2... | collective-permute-start | bytes 2359304 | tf_op jit(solution)/shard_map/ppermute | solution.py:120
  39.9 21.3 %collective-permute-start.8 = (bf16[24,128,128]{2,1,0:T(8,128)(2,1)S(1)}, bf16[24,128,128]{2,1,0:T(8,128)(2,1)}, u32[]{:S(2)}, u32[]{:S(2)}) collective-permute-start(bf16[24,128,128]{2,1,0:T(8,128)(2,1)S(1)} %collective-permute-done.4), channel_id=1, source_target_pairs={{16,8},{20,12},{8,0},{12,4},{17,9},{21,13},{9,1},{13,5},{18,10},{2... | collective-permute-start | bytes 2359304 | tf_op jit(solution)/shard_map/ppermute | solution.py:120
  41.3 21.5 %collective-permute-start.9 = (bf16[24,128,128]{2,1,0:T(8,128)(2,1)S(1)}, bf16[24,128,128]{2,1,0:T(8,128)(2,1)S(1)}, u32[]{:S(2)}, u32[]{:S(2)}) collective-permute-start(bf16[24,128,128]{2,1,0:T(8,128)(2,1)S(1)} %broadcast_select_fusion.5.refs_1_), channel_id=1, source_target_pairs={{0,4},{4,0},{8,12},{12,8},{16,20},{20,16},{24,28},{28,24},{1,5},{5... | collective-permute-start | bytes 2359304 | tf_op jit(solution)/shard_map/ppermute | solution.py:115
  43.5 22.5 %collective-permute-start.11 = (bf16[128,1024]{1,0:T(8,128)(2,1)S(1)}, bf16[128,1024]{1,0:T(8,128)(2,1)S(1)}, u32[]{:S(2)}, u32[]{:S(2)}) collective-permute-start(bf16[128,1024]{1,0:T(8,128)(2,1)S(1)} %convert_element_type.99.refs_8_.refs_0_), channel_id=1, source_target_pairs={{0,1},{1,0},{2,3},{3,2},{4,5},{5,4},{6,7},{7,6},{8,9},{9,8},{10,11... | collective-permute-start | bytes 786440 | tf_op jit(solution)/shard_map/ppermute | solution.py:63
  48.3 17.6 %collective-permute-start.12 = (bf16[128,1024]{1,0:T(8,128)(2,1)S(1)}, bf16[128,1024]{1,0:T(8,128)(2,1)S(1)}, u32[]{:S(2)}, u32[]{:S(2)}) collective-permute-start(bf16[128,1024]{1,0:T(8,128)(2,1)S(1)} %collective-permute-done.10.refs_9_.refs_1_), channel_id=1, source_target_pairs={{0,1},{1,0},{2,3},{3,2},{4,5},{5,4},{6,7},{7,6},{8,9},{9,8},{10,11... | collective-permute-start | bytes 786440 | tf_op jit(solution)/shard_map/ppermute | solution.py:63
  66.5 20.0 %collective-permute-start.13 = (bf16[24,128,128]{2,1,0:T(8,128)(2,1)S(1)}, bf16[24,128,128]{2,1,0:T(8,128)(2,1)S(1)}, u32[]{:S(2)}, u32[]{:S(2)}) collective-permute-start(bf16[24,128,128]{2,1,0:T(8,128)(2,1)S(1)} %copy-done.79), channel_id=1, source_target_pairs={{0,24},{4,28},{24,0},{28,4},{1,25},{5,29},{25,1},{29,5},{2,26},{6,... | collective-permute-start | bytes 2359304 | tf_op jit(solution)/shard_map/ppermute | solution.py:124
  86.6 17.6 %collective-permute-start.19 = (bf16[24,128,128]{2,1,0:T(8,128)(2,1)S(1)}, bf16[24,128,128]{2,1,0:T(8,128)(2,1)}, u32[]{:S(2)}, u32[]{:S(2)}) collective-permute-start(bf16[24,128,128]{2,1,0:T(8,128)(2,1)S(1)} %broadcast_select_fusion.2.refs_3_), channel_id=1, source_target_pairs={{0,4},{4,0},{8,12},{12,8},{16,20},{20,16},{24,28},{28,24},{1,5},{5... | collective-permute-start | bytes 2359304 | tf_op jit(solution)/shard_map/ppermute | solution.py:115
  90.4 17.7 %collective-permute-start.18 = (bf16[24,128,128]{2,1,0:T(8,128)(2,1)}, bf16[24,128,128]{2,1,0:T(8,128)(2,1)}, u32[]{:S(2)}, u32[]{:S(2)}) collective-permute-start(bf16[24,128,128]{2,1,0:T(8,128)(2,1)} %get-tuple-element.157.refs_0_), channel_id=1, source_target_pairs={{8,0},{12,4},{16,8},{20,12},{24,16},{28,20},{9,1},{13,5},{17,9},{2... | collective-permute-start | bytes 2359304 | tf_op jit(solution)/shard_map/ppermute | solution.py:120
  104.2 20.4 %collective-permute-start.22 = (bf16[24,128,128]{2,1,0:T(8,128)(2,1)}, bf16[24,128,128]{2,1,0:T(8,128)(2,1)}, u32[]{:S(2)}, u32[]{:S(2)}) collective-permute-start(bf16[24,128,128]{2,1,0:T(8,128)(2,1)} %get-tuple-element.157.refs_0_), channel_id=1, source_target_pairs={{0,4},{4,0},{8,12},{12,8},{16,20},{20,16},{24,28},{28,24},{1,5},{5... | collective-permute-start | bytes 2359304 | tf_op jit(solution)/shard_map/ppermute | solution.py:115
  129.6 25.5 %collective-permute-start.28 = (bf16[24,128,128]{2,1,0:T(8,128)(2,1)}, bf16[24,128,128]{2,1,0:T(8,128)(2,1)S(1)}, u32[]{:S(2)}, u32[]{:S(2)}) collective-permute-start(bf16[24,128,128]{2,1,0:T(8,128)(2,1)} %get-tuple-element.157.refs_0_), channel_id=1, source_target_pairs={{0,24},{4,28},{24,0},{28,4},{1,25},{5,29},{25,1},{29,5},{2,26},{6,... | collective-permute-start | bytes 2359304 | tf_op jit(solution)/shard_map/ppermute | solution.py:124
  131.6 23.6 %collective-permute-start.29 = (bf16[24,128,128]{2,1,0:T(8,128)(2,1)S(1)}, bf16[24,128,128]{2,1,0:T(8,128)(2,1)S(1)}, u32[]{:S(2)}, u32[]{:S(2)}) collective-permute-start(bf16[24,128,128]{2,1,0:T(8,128)(2,1)S(1)} %broadcast_select_fusion.4.refs_1_), channel_id=1, source_target_pairs={{0,4},{4,0},{8,12},{12,8},{16,20},{20,16},{24,28},{28,24},{1,5},{5... | collective-permute-start | bytes 2359304 | tf_op jit(solution)/shard_map/ppermute | solution.py:115
  159.3 19.6 %collective-permute-start.32 = (bf16[24,128,128]{2,1,0:T(8,128)(2,1)S(1)}, bf16[24,128,128]{2,1,0:T(8,128)(2,1)S(1)}, u32[]{:S(2)}, u32[]{:S(2)}) collective-permute-start(bf16[24,128,128]{2,1,0:T(8,128)(2,1)S(1)} %get-tuple-element.163.refs_2_), channel_id=1, source_target_pairs={{0,4},{4,0},{8,12},{12,8},{16,20},{20,16},{24,28},{28,24},{1,5},{5... | collective-permute-start | bytes 2359304 | tf_op jit(solution)/shard_map/ppermute | solution.py:115
  159.8 31.6 %collective-permute-start.33 = (bf16[24,128,128]{2,1,0:T(8,128)(2,1)}, bf16[24,128,128]{2,1,0:T(8,128)(2,1)}, u32[]{:S(2)}, u32[]{:S(2)}) collective-permute-start(bf16[24,128,128]{2,1,0:T(8,128)(2,1)} %collective-permute-done.22.refs_4_), channel_id=1, source_target_pairs={{0,16},{4,20},{24,8},{28,12},{1,17},{5,21},{25,9},{29,13},{2,18},{... | collective-permute-start | bytes 2359304 | tf_op jit(solution)/shard_map/ppermute | solution.py:210
  164.0 19.0 %collective-permute-start.31 = (bf16[128,1024]{1,0:T(8,128)(2,1)S(1)}, bf16[128,1024]{1,0:T(8,128)(2,1)S(1)}, u32[]{:S(2)}, u32[]{:S(2)}) collective-permute-start(bf16[128,1024]{1,0:T(8,128)(2,1)S(1)} %add_convert_fusion.9), channel_id=1, source_target_pairs={{0,2},{1,3},{2,0},{3,1},{4,6},{5,7},{6,4},{7,5},{8,10},{9,11},{10,... | collective-permute-start | bytes 786440 | tf_op jit(solution)/shard_map/ppermute | solution.py:63
  166.4 25.0 %collective-permute-start.34 = (bf16[12,128,128]{2,1,0:T(8,128)(2,1)}, bf16[12,128,128]{2,1,0:T(8,128)(2,1)}, u32[]{:S(2)}, u32[]{:S(2)}) collective-permute-start(bf16[12,128,128]{2,1,0:T(8,128)(2,1)} %slice.254), channel_id=1, source_target_pairs={{0,24},{4,28},{24,0},{28,4},{1,25},{5,29},{25,1},{29,5},{2,26},{6,... | collective-permute-start | bytes 1179656 | tf_op jit(solution)/shard_map/ppermute | solution.py:124
  384.5 28.1 %collective-permute-start.64 = (bf16[24,128,128]{2,1,0:T(8,128)(2,1)}, bf16[24,128,128]{2,1,0:T(8,128)(2,1)S(1)}, u32[]{:S(2)}, u32[]{:S(2)}) collective-permute-start(bf16[24,128,128]{2,1,0:T(8,128)(2,1)} %get-tuple-element.222), channel_id=1, source_target_pairs={{0,4},{4,0},{8,12},{12,8},{16,20},{20,16},{24,28},{28,24},{1,5},{5... | collective-permute-start | bytes 2359304 | tf_op jit(solution)/shard_map/ppermute | solution.py:115
  385.9 23.1 %collective-permute-start.72 = (bf16[256,1024]{1,0:T(8,128)(2,1)S(1)}, bf16[256,1024]{1,0:T(8,128)(2,1)S(1)}, u32[]{:S(2)}, u32[]{:S(2)}) collective-permute-start(bf16[256,1024]{1,0:T(8,128)(2,1)S(1)} %copy-done.73), channel_id=1, source_target_pairs={{0,1},{1,0},{2,3},{3,2},{4,5},{5,4},{6,7},{7,6},{8,9},{9,8},{10,11... | collective-permute-start | bytes 1572872 | tf_op jit(solution)/shard_map/ppermute | solution.py:63
  412.9 27.5 %collective-permute-start.76 = (bf16[24,128,128]{2,1,0:T(8,128)(2,1)S(1)}, bf16[24,128,128]{2,1,0:T(8,128)(2,1)S(1)}, u32[]{:S(2)}, u32[]{:S(2)}) collective-permute-start(bf16[24,128,128]{2,1,0:T(8,128)(2,1)S(1)} %add_convert_fusion.2), channel_id=1, source_target_pairs={{0,8},{4,12},{8,16},{12,20},{1,9},{5,13},{9,17},{13,21},{2,10},{6,... | collective-permute-start | bytes 2359304 | tf_op jit(solution)/shard_map/ppermute | solution.py:120
  414.3 26.1 %collective-permute-start.77 = (bf16[24,128,128]{2,1,0:T(8,128)(2,1)S(1)}, bf16[24,128,128]{2,1,0:T(8,128)(2,1)S(1)}, u32[]{:S(2)}, u32[]{:S(2)}) collective-permute-start(bf16[24,128,128]{2,1,0:T(8,128)(2,1)S(1)} %add_convert_fusion.2), channel_id=1, source_target_pairs={{24,16},{28,20},{16,8},{20,12},{25,17},{29,21},{17,9},{21,13},{26,... | collective-permute-start | bytes 2359304 | tf_op jit(solution)/shard_map/ppermute | solution.py:120
  415.2 30.9 %collective-permute-start.65 = (f32[2,128,256]{2,1,0:T(8,128)S(1)}, f32[2,128,256]{2,1,0:T(8,128)S(1)}, u32[]{:S(2)}, u32[]{:S(2)}) collective-permute-start(f32[2,128,256]{2,1,0:T(8,128)S(1)} %pad_maximum_fusion.8), channel_id=1, source_target_pairs={{0,1},{1,0},{2,3},{3,2},{4,5},{5,4},{6,7},{7,6},{8,9},{9,8},{10,11... | collective-permute-start | bytes 786440 | tf_op jit(solution)/shard_map/ppermute | solution.py:63
  415.3 22.8 %collective-permute-start.70 = (bf16[24,128,128]{2,1,0:T(8,128)(2,1)S(1)}, bf16[24,128,128]{2,1,0:T(8,128)(2,1)S(1)}, u32[]{:S(2)}, u32[]{:S(2)}) collective-permute-start(bf16[24,128,128]{2,1,0:T(8,128)(2,1)S(1)} %copy-done.107), channel_id=1, source_target_pairs={{0,4},{4,0},{8,12},{12,8},{16,20},{20,16},{24,28},{28,24},{1,5},{5... | collective-permute-start | bytes 2359304 | tf_op jit(solution)/shard_map/ppermute | solution.py:115
  417.2 20.9 %collective-permute-start.78 = (f32[2,12,1024]{2,1,0:T(8,128)S(1)}, f32[2,12,1024]{2,1,0:T(8,128)S(1)}, u32[]{:S(2)}, u32[]{:S(2)}) collective-permute-start(f32[2,12,1024]{2,1,0:T(8,128)S(1)} %add.203), channel_id=1, source_target_pairs={{0,4},{4,0},{8,12},{12,8},{16,20},{20,16},{24,28},{28,24},{1,5},{5... | collective-permute-start | bytes 294920 | tf_op jit(solution)/shard_map/ppermute | solution.py:63
  440.4 18.6 %collective-permute-start.79 = (bf16[24,128,128]{2,1,0:T(8,128)(2,1)S(1)}, bf16[24,128,128]{2,1,0:T(8,128)(2,1)S(1)}, u32[]{:S(2)}, u32[]{:S(2)}) collective-permute-start(bf16[24,128,128]{2,1,0:T(8,128)(2,1)S(1)} %copy-done.106), channel_id=1, source_target_pairs={{0,4},{4,0},{8,12},{12,8},{16,20},{20,16},{24,28},{28,24},{1,5},{5... | collective-permute-start | bytes 2359304 | tf_op jit(solution)/shard_map/ppermute | solution.py:115
  441.8 24.4 %collective-permute-start.80 = (bf16[24,128,128]{2,1,0:T(8,128)(2,1)S(1)}, bf16[24,128,128]{2,1,0:T(8,128)(2,1)S(1)}, u32[]{:S(2)}, u32[]{:S(2)}) collective-permute-start(bf16[24,128,128]{2,1,0:T(8,128)(2,1)S(1)} %add_convert_fusion.1), channel_id=1, source_target_pairs={{0,24},{4,28},{24,0},{28,4},{1,25},{5,29},{25,1},{29,5},{2,26},{6,... | collective-permute-start | bytes 2359304 | tf_op jit(solution)/shard_map/ppermute | solution.py:124
  446.1 22.2 %collective-permute-start.71 = (f32[2,128,256]{2,1,0:T(8,128)S(1)}, f32[2,128,256]{2,1,0:T(8,128)S(1)}, u32[]{:S(2)}, u32[]{:S(2)}) collective-permute-start(f32[2,128,256]{2,1,0:T(8,128)S(1)} %pad_maximum_fusion.9), channel_id=1, source_target_pairs={{0,2},{1,3},{2,0},{3,1},{4,6},{5,7},{6,4},{7,5},{8,10},{9,11},{10,... | collective-permute-start | bytes 786440 | tf_op jit(solution)/shard_map/ppermute | solution.py:63
  459.5 26.8 %collective-permute-start.83 = (bf16[24,128,128]{2,1,0:T(8,128)(2,1)S(1)}, bf16[24,128,128]{2,1,0:T(8,128)(2,1)S(1)}, u32[]{:S(2)}, u32[]{:S(2)}) collective-permute-start(bf16[24,128,128]{2,1,0:T(8,128)(2,1)S(1)} %add_convert_fusion), channel_id=1, source_target_pairs={{0,8},{4,12},{8,16},{12,20},{1,9},{5,13},{9,17},{13,21},{2,10},{6,... | collective-permute-start | bytes 2359304 | tf_op jit(solution)/shard_map/ppermute | solution.py:120
  464.6 21.6 %collective-permute-start.84 = (bf16[24,128,128]{2,1,0:T(8,128)(2,1)S(1)}, bf16[24,128,128]{2,1,0:T(8,128)(2,1)}, u32[]{:S(2)}, u32[]{:S(2)}) collective-permute-start(bf16[24,128,128]{2,1,0:T(8,128)(2,1)S(1)} %add_convert_fusion), channel_id=1, source_target_pairs={{24,16},{28,20},{16,8},{20,12},{25,17},{29,21},{17,9},{21,13},{26,... | collective-permute-start | bytes 2359304 | tf_op jit(solution)/shard_map/ppermute | solution.py:120
  466.2 18.2 %collective-permute-start.81 = (bf16[24,128,128]{2,1,0:T(8,128)(2,1)}, bf16[24,128,128]{2,1,0:T(8,128)(2,1)}, u32[]{:S(2)}, u32[]{:S(2)}) collective-permute-start(bf16[24,128,128]{2,1,0:T(8,128)(2,1)} %get-tuple-element.247), channel_id=1, source_target_pairs={{0,4},{4,0},{8,12},{12,8},{16,20},{20,16},{24,28},{28,24},{1,5},{5... | collective-permute-start | bytes 2359304 | tf_op jit(solution)/shard_map/ppermute | solution.py:115
  467.0 19.2 %collective-permute-start.82 = (bf16[24,128,128]{2,1,0:T(8,128)(2,1)S(1)}, bf16[24,128,128]{2,1,0:T(8,128)(2,1)}, u32[]{:S(2)}, u32[]{:S(2)}) collective-permute-start(bf16[24,128,128]{2,1,0:T(8,128)(2,1)S(1)} %add_convert_fusion.1), channel_id=1, source_target_pairs={{8,0},{12,4},{16,24},{20,28},{9,1},{13,5},{17,25},{21,29},{10,2},{... | collective-permute-start | bytes 2359304 | tf_op jit(solution)/shard_map/ppermute | solution.py:257
  (162 other events, 1795.0 us)
Sparse Core Ops, SparseCore 0:
  306.9 128.1 reduce-scatter.1
